TPU v7x, 512 devices: a whole 4x8x8 slice. The times are simulated.
512 devices in a mesh: row: 32 (over x, z), col: 16 (over y, core).
Axes of the slice: x: 4, y: 8, z: 8, core: 2. Of those that a mesh axis runs over, the one named last changes fastest.
Arguments:
- tiles: bfloat16 [32, 16, 64, 128, 128], P('row', 'col'), may hold values from -0.25 to 0.25
- tile_rows: int32 [32, 16, 64], P('row', 'col'), may hold values from 0 to 127
- tile_cols: int32 [32, 16, 64], P('row', 'col'), may hold values from 0 to 255
- tile_count: int32 [32, 16], P('row', 'col'), may hold values from 1 to 64, as said below
- cost: float32 [524288], P('col'), may hold values from -12 to 12
- upper: float32 [524288], P('col'), may hold values from 0.3 to 4
- var_kind: int32 [524288], P('col'), may hold values from 0 to 2
- rhs: float32 [524288], P('row'), may hold values from -12 to 12
- row_kind: int32 [524288], P('row'), may hold values from 0 to 1
- primal_start: float32 [524288], P('col'), may hold values from -6 to 6
- dual_start: float32 [524288], P('row'), may hold values from -6 to 6
Outputs:
- primal: float32 [524288], P(('col', 'row'))
- dual: float32 [524288], P(('row', 'col'))
- primal_avg: float32 [524288], P(('col', 'row'))
- dual_avg: float32 [524288], P(('row', 'col'))
- objectives: float32 [2], replicated
Inputs may be any that keep to these rules, and one draw needn't show every extreme that they name: `tile_count`: at most 64 live slots on a device; some device has exactly 64.
All inputs are finite; a program needn't handle non-finite values.
Results may differ from a plain program's by a relative error of at most 0.0012.
Values may be sent and summed in bfloat16 or wider, within the bound.
A program may use at most 64 MiB of HBM per device.

v0:
```python
import math

import jax
import jax.numpy as jnp
from jax import lax
from jax.sharding import PartitionSpec as P

TILE = 128
RB = 128
CB = 256
ITERS = 2


primal_step = 0.4
dual_step = 0.4


def project_primal(value, var_kind, upper):
    lower_cut = jnp.where(var_kind == 2, value, jnp.maximum(value, 0.0))
    return jnp.where(var_kind == 0, jnp.minimum(lower_cut, upper), lower_cut)


def project_dual(value, row_kind):
    return jnp.where(row_kind == 1, jnp.maximum(value, 0.0), value)


def body(
    tiles,
    tile_rows,
    tile_cols,
    tile_count,
    cost,
    upper,
    var_kind,
    rhs,
    row_kind,
    primal_start,
    dual_start,
):
    slot_count = tiles.shape[2]
    tile_set = tiles.reshape(slot_count, TILE, TILE)
    block_rows = tile_rows.reshape(-1)
    block_cols = tile_cols.reshape(-1)
    live_mask = (jnp.arange(slot_count, dtype=jnp.int32) < tile_count.reshape(())).astype(
        jnp.float32
    )[:, None]
    row_onehot = (jnp.arange(RB, dtype=jnp.int32)[:, None] == block_rows[None, :]).astype(
        jnp.float32
    )
    col_onehot = (jnp.arange(CB, dtype=jnp.int32)[:, None] == block_cols[None, :]).astype(
        jnp.float32
    )
    primal_len = cost.shape[0] // lax.axis_size("row")
    primal_pos = lax.axis_index("row") * primal_len
    dual_len = rhs.shape[0] // lax.axis_size("col")
    dual_pos = lax.axis_index("col") * dual_len

    def own_primal(values):
        return lax.dynamic_slice_in_dim(values, primal_pos, primal_len)

    def own_dual(values):
        return lax.dynamic_slice_in_dim(values, dual_pos, dual_len)

    cost_used, upper_used, kind_used = (own_primal(cost), own_primal(upper), own_primal(var_kind))
    primal_now = own_primal(primal_start)
    rhs_used, rowkind_used = (own_dual(rhs), own_dual(row_kind))
    dual_now = own_dual(dual_start)
    dual_wide = dual_start.astype(jnp.bfloat16)
    primal_total = jnp.zeros_like(primal_now)
    dual_total = jnp.zeros_like(dual_now)
    for step in range(ITERS):
        blocks = jnp.take(dual_wide.reshape(RB, TILE), block_rows, axis=0)
        products = (
            jnp.einsum("tij,ti->tj", tile_set, blocks, preferred_element_type=jnp.float32)
            * live_mask
        )
        partial_back = jnp.dot(col_onehot, products, precision=lax.Precision.HIGHEST).reshape(-1)
        dual_image = lax.psum_scatter(partial_back, "row", scatter_dimension=0, tiled=True)
        primal_next = project_primal(
            primal_now - primal_step * (cost_used - dual_image), kind_used, upper_used
        )
        extrapolated = (2.0 * primal_next - primal_now).astype(jnp.bfloat16)
        primal_wide = lax.all_gather(extrapolated, "row", axis=0, tiled=True)
        apply_blocks = jnp.take(primal_wide.reshape(CB, TILE), block_cols, axis=0)
        apply_products = (
            jnp.einsum("tij,tj->ti", tile_set, apply_blocks, preferred_element_type=jnp.float32)
            * live_mask
        )
        partial_fore = jnp.dot(row_onehot, apply_products, precision=lax.Precision.HIGHEST).reshape(
            -1
        )
        primal_image = lax.psum_scatter(partial_fore, "col", scatter_dimension=0, tiled=True)
        dual_next = project_dual(dual_now + dual_step * (rhs_used - primal_image), rowkind_used)
        primal_now, dual_now = (primal_next, dual_next)
        primal_total = primal_total + primal_next
        dual_total = dual_total + dual_next
        if step + 1 < ITERS:
            dual_wide = lax.all_gather(dual_next.astype(jnp.bfloat16), "col", axis=0, tiled=True)
    primal_avg = primal_total / ITERS
    dual_avg = dual_total / ITERS
    primal_inner, dual_inner = lax.psum(
        (jnp.sum(own_primal(cost) * primal_avg), jnp.sum(own_dual(rhs) * dual_avg)), ("row", "col")
    )
    total_cols = cost.shape[0] * lax.axis_size("col")
    total_rows = rhs.shape[0] * lax.axis_size("row")
    objectives = jnp.stack(
        [primal_inner / math.sqrt(total_cols), dual_inner / math.sqrt(total_rows)]
    )
    return (primal_now, dual_now, primal_avg, dual_avg, objectives)


def solution(mesh):
    placed = (
        P("row", "col", None, None, None),
        P("row", "col", None),
        P("row", "col", None),
        P("row", "col"),
        P("col"),
        P("col"),
        P("col"),
        P("row"),
        P("row"),
        P("col"),
        P("row"),
    )
    return jax.shard_map(
        body,
        mesh=mesh,
        in_specs=placed,
        out_specs=(P(("col", "row")), P(("row", "col")), P(("col", "row")), P(("row", "col")), P()),
        check_vma=False,
    )
```

profile of v0, /device:TPU:1, one launch (start us, length us, event | category | flops | bytes accessed | tf_op | source)
XLA Modules:
  0.0 757.6 jit_solution(10831349472588626617)
XLA Ops:
  7.2 0.0 copy-start
  7.2 0.0 copy-start.2
  7.2 0.0 all-reduce.10.cloned.1.call-start
  7.2 0.8 compare_and_fusion.1
  8.0 0.7 compare_select_fusion.1
  9.4 0.8 convert_bitcast_fusion
  10.2 0.6 gather_fusion
  10.9 0.1 select_bitcast_fusion.3
  10.9 0.0 copy-done
  10.9 0.0 copy-start.3
  11.0 0.7 fusion.6
  11.6 0.0 copy-done.2
  11.6 0.9 convolution_bitcast_fusion.1
  12.5 0.0 all-reduce.10.cloned.1.call-update
  12.6 0.0 all-reduce.12.cloned.1.call-start
  12.6 1.3 dynamic-slice
  14.6 151.6 %all-reduce.10.cloned.1.call-done = f32[32768]{0:T(1024)} async-done(((f32[32768]{0:T(1024)}), f32[32768]{0:T(1024)}) %all-reduce.10.cloned.1.call-update) | async-done | bytes 131088
  166.2 0.8 subtract_convert_fusion.1
  166.9 34.8 %all_gather.9 = bf16[32768]{0:T(1024)(128)(2,1)S(1)} all-gather(bf16[1024]{0:T(1024)(128)(2,1)S(1)} %get-tuple-element.18), channel_id=1, replica_groups=mesh['row'=32,'col'=16] {'row'}, dimensions={0}, use_global_device_ids=true | all-gather | bytes 67584 | tf_op jit(solution)/shard_map/all_gather | solution.py:83
  201.7 0.6 gather_fusion.1
  202.4 0.1 select_bitcast_fusion.2
  202.5 1.2 fusion.4
  203.6 0.0 copy-done.3
  203.6 0.9 convolution_bitcast_fusion.3
  204.5 0.0 all-reduce.12.cloned.1.call-update
  204.5 0.0 all-reduce.14.cloned.1.call-start
  204.6 1.3 dynamic-slice.2
  206.5 117.8 %all-reduce.12.cloned.1.call-done = f32[16384]{0:T(1024)} async-done(((f32[16384]{0:T(1024)}), f32[16384]{0:T(1024)}) %all-reduce.12.cloned.1.call-update) | async-done | bytes 65552
  324.3 0.7 fusion.32
  325.0 15.2 %all_gather.10 = bf16[16384]{0:T(1024)(128)(2,1)S(1)} all-gather(bf16[1024]{0:T(1024)(128)(2,1)S(1)} %get-tuple-element.15), channel_id=1, replica_groups=mesh['row'=32,'col'=16] {'col'}, dimensions={0}, use_global_device_ids=true | all-gather | bytes 34816 | tf_op jit(solution)/shard_map/all_gather | solution.py:98
  340.2 0.6 gather_fusion.2
  340.8 0.1 select_bitcast_fusion.1
  340.9 0.7 fusion.2
  341.5 0.9 convolution_bitcast_fusion
  342.5 0.0 all-reduce.14.cloned.1.call-update
  342.5 0.0 all-reduce.16.cloned.1.call-start
  342.5 146.8 %all-reduce.14.cloned.1.call-done = f32[32768]{0:T(1024)} async-done(((f32[32768]{0:T(1024)}), f32[32768]{0:T(1024)}) %all-reduce.14.cloned.1.call-update) | async-done | bytes 131088
  489.4 1.9 multiply_reduce_fusion.1
  491.3 0.0 copy-start.1
  491.3 34.8 %all_gather.11 = bf16[32768]{0:T(1024)(128)(2,1)S(1)} all-gather(bf16[1024]{0:T(1024)(128)(2,1)S(1)} %subtract_convert_fusion), channel_id=1, replica_groups=mesh['row'=32,'col'=16] {'row'}, dimensions={0}, use_global_device_ids=true | all-gather | bytes 67584 | tf_op jit(solution)/shard_map/all_gather | solution.py:83
  526.1 0.6 gather_fusion.3
  526.7 0.1 select_bitcast_fusion
  526.8 1.2 fusion
  528.0 0.9 convolution_bitcast_fusion.2
  528.8 0.0 all-reduce.16.cloned.1.call-update
  528.9 119.7 %all-reduce.16.cloned.1.call-done = f32[16384]{0:T(1024)} async-done(((f32[16384]{0:T(1024)}), f32[16384]{0:T(1024)}) %all-reduce.16.cloned.1.call-update) | async-done | bytes 65552
  648.6 1.9 multiply_reduce_fusion
  650.5 98.8 %all-reduce.4 = (f32[]{:T(128)}, f32[]{:T(128)}) all-reduce(f32[]{:T(128)} %get-tuple-element.12, f32[]{:T(128)} %get-tuple-element.9), channel_id=1, replica_groups=mesh['row'=32,'col'=16] {'row','col'}, use_global_device_ids=true, to_apply=%region_7.10 | all-reduce | flops 2 | bytes 16 | tf_op jit(solution)/shard_map/psum | solution.py:101
  750.5 0.6 pad_maximum_fusion
  751.1 0.0 copy-done.1
  (6 shorter events, 0.0 us)
Async XLA Ops:
  7.2 3.8 copy-start
  7.2 4.4 copy-start.2
  7.2 159.0 %all-reduce.10.cloned.1.call-start = ((), (), s32[]{:S(2)}) async-start(), calls=%async_computation | async-start | bytes 262144
  10.9 192.7 %copy-start.3 = (s32[1,1,64]{2,1,0:T(1,128)S(1)}, s32[1,1,64]{2,1,0:T(1,128)}, u32[]{:S(2)}) copy-start(s32[1,1,64]{2,1,0:T(1,128)} %param.16) | copy-start | bytes 772
  12.6 311.7 %all-reduce.12.cloned.1.call-start = ((), (), s32[]{:S(2)}) async-start(), calls=%async_computation.1 | async-start | bytes 131072
  204.5 284.8 %all-reduce.14.cloned.1.call-start = ((), (), s32[]{:S(2)}) async-start(), calls=%async_computation.2 | async-start | bytes 262144
  342.5 306.1 %all-reduce.16.cloned.1.call-start = ((), (), s32[]{:S(2)}) async-start(), calls=%async_computation.3 | async-start | bytes 131072
  491.3 259.8 %copy-start.1 = (f32[1024]{0:T(1024)}, f32[1024]{0:T(1024)S(1)}, u32[]{:S(2)}) copy-start(f32[1024]{0:T(1024)S(1)} %get-tuple-element.11) | copy-start | bytes 12292
Sparse Core Ops, SparseCore 0:
  12.7 153.4 all-reduce.9
  204.7 119.5 all-reduce.11
  342.6 146.7 all-reduce.13
  529.0 119.5 all-reduce.15
where the time goes:
time: 758 us
  waiting for transfers between devices  536 us (71%)
  blocking collectives  184 us (24%)
  between operations  17 us (2%)
  other arithmetic  8.52 us (1%)
    unnamed x8, waiting for transfers between devices  536 us
    psum x1, blocking collectives, body(): lax.psum((jnp.sum(own_primal(cost) * primal_avg), jnp.sum(own_dual(rhs) *...  98.8 us
    all_gather x2, blocking collectives, body(): primal_wide = lax.all_gather(extrapolated, 'row', axis=0, tiled=True)  69.6 us
  transfers between devices with their start and end apart: 4, of which 4 were waited for; matrix products, arithmetic and copies ran while one was open for 0% of the time, Pallas kernels for 0%

commit v1 on v0

v1 whole, which is shorter than its diff:
```python
import functools
import math

import jax
import jax.numpy as jnp
from jax import lax
from jax.experimental import pallas as pl
from jax.experimental.pallas import tpu as pltpu
from jax.sharding import PartitionSpec as P

MESH = pl.DeviceIdType.MESH
TILE = 128
SHARE = 8
GROUP = 16
ITERS = 2
SEND = jnp.bfloat16
PRIMAL_STEP = 0.4
DUAL_STEP = 0.4
BF16 = jnp.bfloat16
F32 = jnp.float32


def project_primal(value, var_kind, upper):
    lower_cut = jnp.where(var_kind == 2, value, jnp.maximum(value, 0.0))
    return jnp.where(var_kind == 0, jnp.minimum(lower_cut, upper), lower_cut)


def project_dual(value, row_kind):
    return jnp.where(row_kind == 1, jnp.maximum(value, 0.0), value)


def zigzag(step, size):
    half = lax.div(step + 1, 2)
    return size // 2 + jnp.where(lax.rem(step, 2) == 0, half, -half)


def split_dot(onehot, products):
    high = products.astype(BF16)
    low = (products - high.astype(F32)).astype(BF16)
    return jnp.dot(onehot, high, preferred_element_type=F32) + jnp.dot(
        onehot, low, preferred_element_type=F32
    )


def kernel(
    sizes,
    tiles_hbm,
    trow_ref,
    tcol_ref,
    count_ref,
    cost_hbm,
    upper_hbm,
    kind_hbm,
    rhs_hbm,
    rkind_hbm,
    primal_hbm,
    dual_hbm,
    out_ref,
    tiles,
    dual_full,
    vecs,
    kinds,
    rs_row_src,
    rs_row_dst,
    ag_row_src,
    ag_row_dst,
    rs_col_src,
    rs_col_dst,
    ag_col_src,
    ag_col_dst,
    obj_col_src,
    obj_col_dst,
    obj_row_src,
    obj_row_dst,
    load_sems,
    send_sems,
    recv_sems,
):
    n_x, n_z, n_y, n_core, slots = sizes
    n_row, n_col = n_x * n_z, n_y * n_core
    me_row = lax.axis_index("row")
    me_col = lax.axis_index("col")
    my_x, my_z = lax.div(me_row, n_z), lax.rem(me_row, n_z)
    my_y, my_core = lax.div(me_col, n_core), lax.rem(me_col, n_core)

    def row_peer(step):
        dz = zigzag(lax.div(step, n_x), n_z)
        dx = zigzag(lax.rem(step, n_x), n_x)
        return lax.rem(my_x + dx, n_x) * n_z + lax.rem(my_z + dz, n_z)

    def col_peer(step):
        dy = zigzag(lax.div(step, n_core), n_y)
        dcore = n_core - 1 - lax.rem(step, n_core)
        return lax.rem(my_y + dy, n_y) * n_core + lax.rem(my_core + dcore, n_core)

    barrier = pltpu.get_barrier_semaphore()

    @pl.loop(0, n_row - 1)
    def _(step):
        pl.semaphore_signal(
            barrier, inc=1, device_id={"row": row_peer(step)}, device_id_type=MESH
        )

    @pl.loop(0, n_col - 1)
    def _(step):
        pl.semaphore_signal(
            barrier, inc=1, device_id={"col": col_peer(step)}, device_id_type=MESH
        )

    row_share = pl.ds(pl.multiple_of(me_row * SHARE, SHARE), SHARE)
    col_share = pl.ds(pl.multiple_of(me_col * SHARE, SHARE), SHARE)
    loads = [
        pltpu.make_async_copy(dual_hbm, dual_full, load_sems.at[0]),
        pltpu.make_async_copy(tiles_hbm, tiles, load_sems.at[1]),
        pltpu.make_async_copy(cost_hbm.at[row_share], vecs.at[0], load_sems.at[2]),
        pltpu.make_async_copy(upper_hbm.at[row_share], vecs.at[1], load_sems.at[3]),
        pltpu.make_async_copy(primal_hbm.at[row_share], vecs.at[2], load_sems.at[4]),
        pltpu.make_async_copy(rhs_hbm.at[col_share], vecs.at[3], load_sems.at[5]),
        pltpu.make_async_copy(dual_hbm.at[col_share], vecs.at[4], load_sems.at[6]),
        pltpu.make_async_copy(kind_hbm.at[row_share], kinds.at[0], load_sems.at[7]),
        pltpu.make_async_copy(rkind_hbm.at[col_share], kinds.at[1], load_sems.at[8]),
    ]
    for load in loads:
        load.start()

    n_rblocks, n_cblocks = n_col * SHARE, n_row * SHARE
    live = lax.broadcasted_iota(jnp.int32, (1, slots), 1) < count_ref[0, 0]
    block_rows = jnp.where(live, trow_ref[...], -1)
    block_cols = jnp.where(live, tcol_ref[...], -1)
    row_hot = (
        lax.broadcasted_iota(jnp.int32, (n_rblocks, slots), 0) == block_rows
    ).astype(F32)
    col_hot = (
        lax.broadcasted_iota(jnp.int32, (n_cblocks, slots), 0) == block_cols
    ).astype(F32)
    row_pick, col_pick = row_hot.T.astype(BF16), col_hot.T.astype(BF16)
    row_put, col_put = row_hot.astype(BF16), col_hot.astype(BF16)
    sub = lax.broadcasted_iota(jnp.int32, (GROUP, TILE), 0)

    def back(dual_wide):
        picked = jnp.dot(row_pick, dual_wide, preferred_element_type=F32)
        products = []
        for g in range(slots // GROUP):
            part = picked[g * GROUP : (g + 1) * GROUP]
            spread = jnp.concatenate(
                [jnp.where(sub == j, part, 0.0).astype(BF16) for j in range(GROUP)], axis=1
            )
            block = tiles[g * GROUP : (g + 1) * GROUP].reshape(GROUP * TILE, TILE)
            products.append(jnp.dot(spread, block, preferred_element_type=F32))
        return split_dot(col_put, jnp.concatenate(products, axis=0))

    def fore(primal_wide):
        picked = jnp.dot(col_pick, primal_wide, preferred_element_type=F32).astype(BF16)
        products = []
        for g in range(slots // GROUP):
            part = picked[g * GROUP : (g + 1) * GROUP]
            block = tiles[g * GROUP : (g + 1) * GROUP].reshape(GROUP * TILE, TILE)
            every = lax.dot_general(
                part, block, (((1,), (1,)), ((), ())), preferred_element_type=F32
            )
            own = jnp.zeros((GROUP, TILE), F32)
            for j in range(GROUP):
                own = own + jnp.where(sub == j, every[:, j * TILE : (j + 1) * TILE], 0.0)
            products.append(own)
        return split_dot(row_put, jnp.concatenate(products, axis=0))

    pending = []

    def exchange(axis, phase, source, dest, scatter):
        n, me, peer_of = (
            (n_row, me_row, row_peer) if axis == "row" else (n_col, me_col, col_peer)
        )

        @pl.loop(0, n - 1)
        def _(step):
            peer = peer_of(step)
            pltpu.make_async_remote_copy(
                src_ref=source.at[peer] if scatter else source,
                dst_ref=dest.at[me],
                send_sem=send_sems.at[phase],
                recv_sem=recv_sems.at[phase],
                device_id={axis: peer},
                device_id_type=MESH,
            ).start()

        dest[me] = source[me] if scatter else source[...]
        both = dest.at[pl.ds(0, n - 1)]
        pltpu.make_async_copy(both, both, recv_sems.at[phase]).wait()
        pending.append((both, phase))
        return dest[...]

    for load in loads[:2]:
        load.wait()
    partial = back(dual_full[...].astype(BF16))
    rs_row_src[0] = partial.reshape(n_row, SHARE, TILE).astype(SEND)
    for load in loads[2:]:
        load.wait()
    cost, upper, primal_now, rhs, dual_now = (vecs[i] for i in range(5))
    var_kind, row_kind = kinds[0], kinds[1]
    pl.semaphore_wait(barrier, n_row + n_col - 2)

    primal_total = jnp.zeros_like(primal_now)
    dual_total = jnp.zeros_like(dual_now)
    phase = 0
    for it in range(ITERS):
        got = exchange("row", phase, rs_row_src.at[it], rs_row_dst.at[it], True)
        phase += 1
        dual_image = jnp.sum(got.astype(F32), axis=0)
        primal_next = project_primal(
            primal_now - PRIMAL_STEP * (cost - dual_image), var_kind, upper
        )
        ag_row_src[it] = (2.0 * primal_next - primal_now).astype(BF16)
        got = exchange("row", phase, ag_row_src.at[it], ag_row_dst.at[it], False)
        phase += 1
        wide = got.astype(F32).reshape(n_cblocks, TILE).astype(BF16)
        rs_col_src[it] = fore(wide).reshape(n_col, SHARE, TILE).astype(SEND)
        got = exchange("col", phase, rs_col_src.at[it], rs_col_dst.at[it], True)
        phase += 1
        primal_image = jnp.sum(got.astype(F32), axis=0)
        dual_next = project_dual(dual_now + DUAL_STEP * (rhs - primal_image), row_kind)
        primal_now, dual_now = primal_next, dual_next
        primal_total = primal_total + primal_next
        dual_total = dual_total + dual_next
        if it + 1 < ITERS:
            ag_col_src[it] = dual_next.astype(BF16)
            got = exchange("col", phase, ag_col_src.at[it], ag_col_dst.at[it], False)
            phase += 1
            wide = got.astype(F32).reshape(n_rblocks, TILE).astype(BF16)
            rs_row_src[it + 1] = back(wide).reshape(n_row, SHARE, TILE).astype(SEND)

    primal_avg, dual_avg = primal_total / ITERS, dual_total / ITERS
    obj_col_src[0:1] = jnp.sum(cost * primal_avg, axis=0, keepdims=True)
    obj_col_src[1:2] = jnp.sum(rhs * dual_avg, axis=0, keepdims=True)
    got = exchange("col", phase, obj_col_src, obj_col_dst, False)
    phase += 1
    obj_row_src[...] = jnp.sum(got, axis=0)
    got = exchange("row", phase, obj_row_src, obj_row_dst, False)
    inner = jnp.sum(jnp.sum(got, axis=0), axis=1, keepdims=True)
    primal_scale = 1.0 / math.sqrt(n_cblocks * TILE * n_col)
    dual_scale = 1.0 / math.sqrt(n_rblocks * TILE * n_row)
    first = lax.broadcasted_iota(jnp.int32, (SHARE, TILE), 1) == 0
    out_ref[0] = primal_now
    out_ref[1] = dual_now
    out_ref[2] = primal_avg
    out_ref[3] = dual_avg
    out_ref[4] = jnp.where(first, inner[0:1] * primal_scale, inner[1:2] * dual_scale)
    for both, which in pending:
        pltpu.make_async_copy(both, both, send_sems.at[which]).wait()


def split_kernel(packed_ref, *out_refs):
    for i in range(4):
        out_refs[i][...] = packed_ref[i]
    out_refs[4][...] = packed_ref[4]


def solution(mesh):
    n_row, n_col = mesh.shape["row"], mesh.shape["col"]
    n_x, n_core = 4, 2
    n_z, n_y = n_row // n_x, n_col // n_core

    def body(
        tiles,
        tile_rows,
        tile_cols,
        tile_count,
        cost,
        upper,
        var_kind,
        rhs,
        row_kind,
        primal_start,
        dual_start,
    ):
        slots = tiles.shape[2]
        sizes = (n_x, n_z, n_y, n_core, slots)
        n_rblocks, n_cblocks = n_col * SHARE, n_row * SHARE
        anywhere = pl.BlockSpec(memory_space=pl.ANY)
        vmem = pl.BlockSpec(memory_space=pltpu.VMEM)
        smem = pl.BlockSpec(memory_space=pltpu.SMEM)
        n_phases = 4 * ITERS + 1
        packed = pl.pallas_call(
            functools.partial(kernel, sizes),
            out_shape=jax.ShapeDtypeStruct((5, SHARE, TILE), F32),
            in_specs=[anywhere, vmem, vmem, smem] + [anywhere] * 7,
            out_specs=vmem,
            scratch_shapes=[
                pltpu.VMEM((slots, TILE, TILE), BF16),
                pltpu.VMEM((n_rblocks, TILE), F32),
                pltpu.VMEM((5, SHARE, TILE), F32),
                pltpu.VMEM((2, SHARE, TILE), jnp.int32),
                pltpu.VMEM((ITERS, n_row, SHARE, TILE), SEND),
                pltpu.VMEM((ITERS, n_row, SHARE, TILE), SEND),
                pltpu.VMEM((ITERS, SHARE, TILE), BF16),
                pltpu.VMEM((ITERS, n_row, SHARE, TILE), BF16),
                pltpu.VMEM((ITERS, n_col, SHARE, TILE), SEND),
                pltpu.VMEM((ITERS, n_col, SHARE, TILE), SEND),
                pltpu.VMEM((ITERS - 1, SHARE, TILE), BF16),
                pltpu.VMEM((ITERS - 1, n_col, SHARE, TILE), BF16),
                pltpu.VMEM((2, TILE), F32),
                pltpu.VMEM((n_col, 2, TILE), F32),
                pltpu.VMEM((2, TILE), F32),
                pltpu.VMEM((n_row, 2, TILE), F32),
                pltpu.SemaphoreType.DMA((9,)),
                pltpu.SemaphoreType.DMA((n_phases,)),
                pltpu.SemaphoreType.DMA((n_phases,)),
            ],
            compiler_params=pltpu.CompilerParams(
                collective_id=0, has_side_effects=True, vmem_limit_bytes=60 * 2**20
            ),
            name="pdhg",
        )(
            tiles.reshape(slots, TILE, TILE),
            tile_rows.reshape(1, slots),
            tile_cols.reshape(1, slots),
            tile_count,
            cost.reshape(n_cblocks, TILE),
            upper.reshape(n_cblocks, TILE),
            var_kind.reshape(n_cblocks, TILE),
            rhs.reshape(n_rblocks, TILE),
            row_kind.reshape(n_rblocks, TILE),
            primal_start.reshape(n_cblocks, TILE),
            dual_start.reshape(n_rblocks, TILE),
        )
        share = jax.ShapeDtypeStruct((SHARE, TILE), F32)
        outs = pl.pallas_call(
            split_kernel,
            out_shape=(share,) * 5,
            in_specs=[vmem],
            out_specs=(vmem,) * 5,
            name="unpack",
        )(packed)
        return tuple(o.reshape(-1) for o in outs[:4]) + (outs[4][0, :2],)

    placed = (
        P("row", "col", None, None, None),
        P("row", "col", None),
        P("row", "col", None),
        P("row", "col"),
        P("col"),
        P("col"),
        P("col"),
        P("row"),
        P("row"),
        P("col"),
        P("row"),
    )
    return jax.shard_map(
        body,
        mesh=mesh,
        in_specs=placed,
        out_specs=(P(("col", "row")), P(("row", "col")), P(("col", "row")), P(("row", "col")), P()),
        check_vma=False,
    )
```

time: 758 us -> 70.6 us (0.09)
  waiting for transfers between devices: 536 us -> 0 us
  blocking collectives: 184 us -> 0 us
  Pallas kernels: 0 us -> 67.8 us
  between operations: 17 us -> 1.29 us
  other arithmetic: 8.52 us -> 0 us
    unnamed x8 -> x0, waiting for transfers between devices: 536 us -> none
    psum x1 -> x0, blocking collectives: 98.8 us -> none  [body(): lax.psum((jnp.sum(own_primal(cost) * primal_avg), jnp.sum(own_dual(rhs) *...]
    all_gather x3 -> x0, blocking collectives: 84.7 us -> none  [the longest x2 69.6 us: body(): primal_wide = lax.all_gather(extrapolated, 'row', axis=0, tiled=True)]
    pallas_call x0 -> x2, Pallas kernels: none -> 67.8 us  [the longest x1 66.5 us: body(): pl.pallas_call(functools.partial(kernel, sizes), out_shape=jax.ShapeDtype...]
  transfers between devices with their start and end apart: 4 -> 0, of which waited for: 4 -> 0; matrix products, arithmetic and copies ran while one was open for 0% -> 0% of each run, Pallas kernels for 0% -> 0%
where the time goes in v1:
time: 70.6 us; the launch traced here: 70.3 us
  Pallas kernels  67.8 us (96%)
  between operations  1.29 us (2%)
  local copies, waits for them, and re-layouts  1.19 us (2%)
    pallas_call x1, Pallas kernels, body(): pl.pallas_call(functools.partial(kernel, sizes), out_shape=jax.ShapeDtype...  66.5 us

profile of v1, /device:TPU:1, one launch (start us, length us, event | category | flops | bytes accessed | tf_op | source)
XLA Modules:
  0.0 70.3 jit_solution(9850360602232851505)
XLA Ops:
  1.3 66.5 %pdhg.1.packed_ref = f32[5,8,128]{2,1,0:T(8,128)} custom-call(bf16[64,128,128]{2,1,0:T(8,128)(2,1)} %bitcast.16, s32[1,64]{1,0:T(1,128)} %bitcast.24, s32[1,64]{1,0:T(1,128)} %bitcast.25, s32[1,1]{1,0:T(1,128)S(6)} %copy.16.count_ref, f32[256,128]{1,0:T(8,128)} %bitcast.17, f32[256,128]{1,0:T(8,128)} %bitcast.18, s32[256,128]{1,0:T(8,128)} %bitcast.19, ...), custom_call_target="tpu_custom_call" | custom-call | tf_op jit(solution)/shard_map/pdhg/pallas_call | solution.py:282
  67.8 1.3 %unpack.1 = (f32[8,128]{1,0:T(8,128)}, f32[8,128]{1,0:T(8,128)}, f32[8,128]{1,0:T(8,128)}, f32[8,128]{1,0:T(8,128)}, f32[8,128]{1,0:T(8,128)}) custom-call(f32[5,8,128]{2,1,0:T(8,128)} %pdhg.1.packed_ref), custom_call_target="tpu_custom_call" | custom-call | tf_op jit(solution)/shard_map/unpack/pallas_call | solution.py:326
  69.1 1.2 %slice_bitcast_fusion = f32[2]{0:T(128)} fusion(f32[8,128]{1,0:T(8,128)} %get-tuple-element.14), kind=kLoop, calls=%fused_computation | loop fusion | bytes 16 | tf_op jit(solution)/shard_map/squeeze | solution.py:333

commit v2 on v1

v2 whole, which is shorter than its diff:
```python
import functools
import math

import jax
import jax.numpy as jnp
from jax import lax
from jax.experimental import pallas as pl
from jax.experimental.pallas import tpu as pltpu
from jax.sharding import PartitionSpec as P

MESH = pl.DeviceIdType.MESH
TILE = 128
SHARE = 8
GROUP = 16
ITERS = 2
N_X = 4
N_CORE = 2
LEVELS = 32767.0
PRIMAL_STEP = 0.4
DUAL_STEP = 0.4
BF16 = jnp.bfloat16
F32 = jnp.float32
I32 = jnp.int32
I16 = jnp.int16
SEMS = 24


def project_primal(value, var_kind, upper):
    lower_cut = jnp.where(var_kind == 2, value, jnp.maximum(value, 0.0))
    return jnp.where(var_kind == 0, jnp.minimum(lower_cut, upper), lower_cut)


def project_dual(value, row_kind):
    return jnp.where(row_kind == 1, jnp.maximum(value, 0.0), value)


def zigzag(step, size):
    half = lax.div(step + 1, 2)
    return size // 2 + jnp.where(lax.rem(step, 2) == 0, half, -half)


def twice(row):
    wide = jnp.broadcast_to(row, (8, TILE))
    lane = lax.broadcasted_iota(I32, wide.shape, 1)
    return jnp.where(lane < TILE // 2, wide, pltpu.roll(wide, TILE // 2, 1))


def quantize(sums):
    top = jnp.max(jnp.abs(sums), axis=-2, keepdims=True)
    inverse = LEVELS / jnp.maximum(top, 1e-30)
    return jnp.round(sums * inverse).astype(I32).astype(I16), top * (1.0 / LEVELS)


def kernel(
    sizes,
    tiles_hbm,
    trow_hbm,
    tcol_hbm,
    count_ref,
    cost_hbm,
    upper_hbm,
    kind_hbm,
    rhs_hbm,
    rkind_hbm,
    primal_hbm,
    dual_hbm,
    out_ref,
    tiles,
    raw_idx,
    col_vecs,
    col_kind,
    row_vecs,
    row_kind_full,
    idx_src,
    idx_x,
    idx_z,
    idx_y,
    idx_c,
    match_z,
    match_y,
    px_src,
    px_dst,
    zq_src,
    zq_dst,
    zs_src,
    zs_dst,
    zo_src,
    zo_dst,
    pc_src,
    pc_dst,
    yq_src,
    yq_dst,
    ys_src,
    ys_dst,
    yo_src,
    yo_dst,
    lq_src,
    ls_src,
    mid_src,
    mid_dst,
    po_src,
    po_dst,
    last_y,
    fin_src,
    fin_dst,
    load_sems,
    send_sems,
    recv_sems,
):
    n_x, n_z, n_y, n_core, slots = sizes
    n_row, n_col = n_x * n_z, n_y * n_core
    n_rblocks, n_cblocks = n_col * SHARE, n_row * SHARE
    me_row = lax.axis_index("row")
    me_col = lax.axis_index("col")
    my_x, my_z = lax.div(me_row, n_z), lax.rem(me_row, n_z)
    my_y, my_core = lax.div(me_col, n_core), lax.rem(me_col, n_core)

    def x_peer(step):
        at = lax.rem(my_x + zigzag(step, n_x), n_x)
        return at, (at * n_z + my_z, me_col)

    def z_peer(step):
        at = lax.rem(my_z + zigzag(step, n_z), n_z)
        return at, (my_x * n_z + at, me_col)

    def y_peer(step):
        at = lax.rem(my_y + zigzag(step, n_y), n_y)
        return at, (me_row, at * n_core + my_core)

    def core_peer(step):
        at = lax.rem(my_core + 1 + step, n_core)
        return at, (me_row, my_y * n_core + at)

    def last_peer(step):
        ahead = lax.div(step, n_core)
        at_z = lax.rem(my_z + zigzag(lax.div(ahead, n_x), n_z), n_z)
        at_x = lax.rem(my_x + zigzag(lax.rem(ahead, n_x), n_x), n_x)
        at_core = lax.rem(my_core + n_core - 1 - lax.rem(step, n_core), n_core)
        return step, (at_x * n_z + at_z, my_y * n_core + at_core)

    barrier = pltpu.get_barrier_semaphore()
    n_last = n_row * n_core

    @pl.loop(0, n_last - 1)
    def _(step):
        pl.semaphore_signal(barrier, inc=1, device_id=last_peer(step)[1], device_id_type=MESH)

    @pl.loop(0, n_y - 1)
    def _(step):
        pl.semaphore_signal(barrier, inc=1, device_id=y_peer(step)[1], device_id_type=MESH)

    n_groups = slots // GROUP
    pieces = [pl.ds(g * GROUP, GROUP) for g in range(n_groups)]
    first_loads = [
        (trow_hbm, raw_idx.at[0]),
        (tcol_hbm, raw_idx.at[1]),
        (dual_hbm, row_vecs.at[0]),
    ]
    tile_loads = [(tiles_hbm.at[piece], tiles.at[piece]) for piece in pieces]
    late_loads = [
        (primal_hbm, col_vecs.at[0]),
        (cost_hbm, col_vecs.at[1]),
        (upper_hbm, col_vecs.at[2]),
        (kind_hbm, col_kind),
        (rhs_hbm, row_vecs.at[1]),
        (rkind_hbm, row_kind_full),
    ]
    copies = [
        pltpu.make_async_copy(src, dst, load_sems.at[i])
        for i, (src, dst) in enumerate(first_loads + tile_loads + late_loads)
    ]
    for copy in copies:
        copy.start()
    n_first, n_tile = len(first_loads), len(tile_loads)
    for copy in copies[:n_first]:
        copy.wait()

    live = lax.broadcasted_iota(I32, (1, slots), 1) < count_ref[0, 0]
    block_rows = jnp.where(live, raw_idx[0], -1)
    block_cols = jnp.where(live, raw_idx[1], -1)
    row_pick = (
        (lax.broadcasted_iota(I32, (n_rblocks, slots), 0) == block_rows).astype(F32).T
    )
    sub = lax.broadcasted_iota(I32, (GROUP, TILE), 0)

    def back(part_of, ready):
        products = []
        for g in range(n_groups):
            ready(g)
            part = part_of[g * GROUP : (g + 1) * GROUP]
            spread = jnp.concatenate(
                [jnp.where(sub == j, part, 0.0).astype(BF16) for j in range(GROUP)], axis=1
            )
            block = tiles[g * GROUP : (g + 1) * GROUP].reshape(GROUP * TILE, TILE)
            products.append(jnp.dot(spread, block, preferred_element_type=F32))
        return jnp.concatenate(products, axis=0)

    def fore(part_of):
        products = []
        for g in range(n_groups):
            part = part_of[g * GROUP : (g + 1) * GROUP]
            block = tiles[g * GROUP : (g + 1) * GROUP].reshape(GROUP * TILE, TILE)
            every = lax.dot_general(
                part, block, (((1,), (1,)), ((), ())), preferred_element_type=F32
            )
            own = jnp.zeros((GROUP, TILE), F32)
            for j in range(GROUP):
                own = own + jnp.where(sub == j, every[:, j * TILE : (j + 1) * TILE], 0.0)
            products.append(own)
        return jnp.concatenate(products, axis=0)

    pending = []
    used = [0]

    def send(peer, count, source, dest, slot):
        sem = used[0]
        used[0] += 1

        @pl.loop(0, count)
        def _(step):
            at, device = peer(step)
            pltpu.make_async_remote_copy(
                src_ref=source(at),
                dst_ref=dest.at[slot],
                send_sem=send_sems.at[sem],
                recv_sem=recv_sems.at[sem],
                device_id=device,
                device_id_type=MESH,
            ).start()

        both = dest.at[pl.ds(0, count)]
        pending.append((both, sem))

        def arrive():
            pltpu.make_async_copy(both, both, recv_sems.at[sem]).wait()

        return arrive

    def put_split(ref, products):
        high = products.astype(BF16)
        ref[0:slots] = high
        ref[slots : 2 * slots] = (products - high.astype(F32)).astype(BF16)

    rounded = row_vecs[0].astype(BF16)
    picked = jnp.dot(row_pick.astype(BF16), rounded, preferred_element_type=F32)
    put_split(px_src.at[0], back(picked, lambda g: copies[n_first + g].wait()))
    idx_src[...] = jnp.full((2, TILE), -1, I32)
    idx_src[0:1, 0:slots] = block_cols
    idx_src[1:2, 0:slots] = block_rows
    pl.semaphore_wait(barrier, n_last - 1 + n_y - 1)

    z_idx_in = send(z_peer, n_z - 1, lambda at: idx_src, idx_z, my_z)
    x_idx_in = send(x_peer, n_x - 1, lambda at: idx_src, idx_x, my_x)
    x_in = send(x_peer, n_x - 1, lambda at: px_src.at[0], px_dst.at[0], my_x)
    y_idx_in = send(y_peer, n_y - 1, lambda at: idx_src, idx_y, my_y)
    c_idx_in = send(core_peer, n_core - 1, lambda at: idx_src, idx_c, my_core)
    for mine, ref in ((my_x, idx_x), (my_z, idx_z), (my_y, idx_y), (my_core, idx_c)):
        ref[mine] = idx_src[...]
    px_dst[0, my_x] = px_src[0]

    for copy in copies[n_first + n_tile :]:
        copy.wait()
    col_pick = (
        (lax.broadcasted_iota(I32, (n_cblocks, slots), 0) == block_cols).astype(F32).T
    )
    col_all = jnp.concatenate(
        [col_vecs[0], col_vecs[1], col_vecs[2], col_kind[...].astype(F32)], axis=1
    )
    col_got = jnp.dot(
        col_pick, col_all, precision=lax.Precision.HIGHEST, preferred_element_type=F32
    )
    x_need, cost_need, upper_need, kind_need = (
        col_got[:, i * TILE : (i + 1) * TILE] for i in range(4)
    )
    row_all = jnp.concatenate(
        [row_vecs[0], row_vecs[1], row_kind_full[...].astype(F32)], axis=1
    )
    row_got = jnp.dot(
        row_pick, row_all, precision=lax.Precision.HIGHEST, preferred_element_type=F32
    )
    y_need, rhs_need, rkind_need = (row_got[:, i * TILE : (i + 1) * TILE] for i in range(3))
    row_share = pl.ds(pl.multiple_of(me_row * SHARE, SHARE), SHARE)
    col_share = pl.ds(pl.multiple_of(me_col * SHARE, SHARE), SHARE)
    x_own, cost_own, upper_own = (col_vecs[i, row_share] for i in range(3))
    kind_own = col_kind[row_share]
    y_own, rhs_own, rkind_own = row_vecs[0, col_share], row_vecs[1, col_share], row_kind_full[col_share]

    z_idx_in()
    x_idx_in()
    need_cols = idx_z[:, 0, :].astype(F32).T[:slots]
    own_cols = lax.broadcasted_iota(I32, (n_z * SHARE, TILE), 0) + my_x * (n_z * SHARE)
    for k in range(n_x):
        have = twice(idx_x[k, 0:1])
        lanes = slice(k * TILE, (k + 1) * TILE)
        have_wide = jnp.broadcast_to(have[0:1], (slots, TILE)).astype(F32)
        for z in range(n_z):
            match_z[z * slots : (z + 1) * slots, lanes] = jnp.where(
                need_cols[:, z : z + 1] == have_wide, 1.0, 0.0
            ).astype(BF16)
        match_z[n_z * slots :, lanes] = jnp.where(own_cols == have[0:1], 1.0, 0.0).astype(BF16)
    y_idx_in()
    c_idx_in()
    need_rows = idx_y[:, 1, :].astype(F32).T[:slots]
    own_at = lax.broadcasted_iota(I32, (n_y * SHARE, TILE), 0)
    own_rows = (lax.div(own_at, SHARE) * n_core + my_core) * SHARE + lax.rem(own_at, SHARE)
    for k in range(n_core):
        have = twice(idx_c[k, 1:2])
        lanes = slice(k * TILE, (k + 1) * TILE)
        have_wide = jnp.broadcast_to(have[0:1], (slots, TILE)).astype(F32)
        for y in range(n_y):
            match_y[y * slots : (y + 1) * slots, lanes] = jnp.where(
                need_rows[:, y : y + 1] == have_wide, 1.0, 0.0
            ).astype(BF16)
        match_y[n_y * slots :, lanes] = jnp.where(own_rows == have[0:1], 1.0, 0.0).astype(BF16)

    def total(levels, scales):
        return jnp.sum(levels.astype(F32) * scales, axis=0)

    n_zneed, n_yneed = n_z * slots, n_y * slots
    x_total = jnp.zeros_like(x_own)
    y_first = y_own
    for it in range(ITERS):
        last = it + 1 == ITERS
        x_in()
        sums = jnp.dot(
            match_z[...],
            px_dst[it].reshape(n_x * 2 * slots, TILE),
            preferred_element_type=F32,
        )
        zq_src[it], zs_src[it] = quantize(sums[:n_zneed].reshape(n_z, slots, TILE))
        zq_in = send(z_peer, n_z - 1, lambda at: zq_src.at[it, at], zq_dst.at[it], my_z)
        zs_in = send(z_peer, n_z - 1, lambda at: zs_src.at[it, at], zs_dst.at[it], my_z)
        zo_src[it] = sums[n_zneed:].reshape(n_z, SHARE, TILE)
        zo_in = send(z_peer, n_z - 1, lambda at: zo_src.at[it, at], zo_dst.at[it], my_z)
        zq_dst[it, my_z] = zq_src[it, my_z]
        zs_dst[it, my_z] = zs_src[it, my_z]
        zo_dst[it, my_z] = zo_src[it, my_z]
        if it > 0:
            yo_in()
            y_first = project_dual(
                y_own + DUAL_STEP * (rhs_own - jnp.sum(yo_dst[...], axis=0)), rkind_own
            )
            mid_src[...] = y_first
            mid_in = send(y_peer, n_y - 1, lambda at: mid_src, mid_dst, my_y)
            mid_dst[my_y] = y_first
        zq_in()
        zs_in()
        x_new = project_primal(
            x_need - PRIMAL_STEP * (cost_need - total(zq_dst[it], zs_dst[it])),
            kind_need,
            upper_need,
        )
        put_split(pc_src.at[it], fore((2.0 * x_new - x_need).astype(BF16)))
        x_need = x_new
        c_in = send(core_peer, n_core - 1, lambda at: pc_src.at[it], pc_dst.at[it], my_core)
        pc_dst[it, my_core] = pc_src[it]
        zo_in()
        x_own = project_primal(
            x_own - PRIMAL_STEP * (cost_own - jnp.sum(zo_dst[it], axis=0)), kind_own, upper_own
        )
        x_total = x_total + x_own
        c_in()
        parts = pc_dst[it].reshape(n_core * 2 * slots, TILE)
        if not last:
            sums = jnp.dot(match_y[...], parts, preferred_element_type=F32)
            yq_src[...], ys_src[...] = quantize(sums[:n_yneed].reshape(n_y, slots, TILE))
            yq_in = send(y_peer, n_y - 1, lambda at: yq_src.at[at], yq_dst.at[it], my_y)
            ys_in = send(y_peer, n_y - 1, lambda at: ys_src.at[at], ys_dst.at[it], my_y)
            yo_src[...] = sums[n_yneed:].reshape(n_y, SHARE, TILE)
            yo_in = send(y_peer, n_y - 1, lambda at: yo_src.at[at], yo_dst, my_y)
            yq_dst[it, my_y] = yq_src[my_y]
            ys_dst[it, my_y] = ys_src[my_y]
            yo_dst[my_y] = yo_src[my_y]
            yq_in()
            ys_in()
            y_need = project_dual(
                y_need + DUAL_STEP * (rhs_need - total(yq_dst[it], ys_dst[it])), rkind_need
            )
            put_split(
                px_src.at[it + 1], back(y_need.astype(BF16).astype(F32), lambda g: None)
            )
            x_in = send(x_peer, n_x - 1, lambda at: px_src.at[it + 1], px_dst.at[it + 1], my_x)
            px_dst[it + 1, my_x] = px_src[it + 1]

    sums = jnp.dot(match_y[n_yneed:], parts, preferred_element_type=F32)
    lq_src[...], ls_src[...] = quantize(sums)
    yq_in = send(y_peer, n_y - 1, lambda at: lq_src, yq_dst.at[ITERS - 1], my_y)
    ys_in = send(y_peer, n_y - 1, lambda at: ls_src, ys_dst.at[ITERS - 1], my_y)
    primal_avg = x_total / ITERS
    po_src[...] = jnp.sum(cost_own * primal_avg, axis=0, keepdims=True)
    po_in = send(y_peer, n_y - 1, lambda at: po_src, po_dst, my_y)
    yq_dst[ITERS - 1, my_y] = lq_src[...]
    ys_dst[ITERS - 1, my_y] = ls_src[...]
    po_dst[my_y] = po_src[...]
    half_rhs = row_vecs[1].reshape(n_y, n_core, SHARE, TILE)
    half_kind = row_kind_full[...].reshape(n_y, n_core, SHARE, TILE)

    def of_core(both):
        one = both[:, 0]
        for k in range(1, n_core):
            one = jnp.where(my_core == k, both[:, k], one)
        return one.reshape(n_y * SHARE, TILE)

    half_rhs, half_kind = of_core(half_rhs), of_core(half_kind)
    mid_in()
    half_y = mid_dst[...].reshape(n_y * SHARE, TILE)
    po_in()
    fin_src[0:1] = jnp.sum(po_dst[...], axis=0)
    yq_in()
    ys_in()
    half_new = project_dual(
        half_y + DUAL_STEP * (half_rhs - total(yq_dst[ITERS - 1], ys_dst[ITERS - 1])), half_kind
    )
    half_avg = (half_y + half_new) / ITERS
    fin_src[1:2] = jnp.sum(half_rhs * half_avg, axis=0, keepdims=True)
    me_last = me_row * n_core + my_core
    fin_in = send(last_peer, n_last - 1, lambda at: fin_src, fin_dst, me_last)
    fin_dst[me_last] = fin_src[...]
    last_y[0] = half_new
    last_y[1] = half_avg
    mine = pl.ds(pl.multiple_of(my_y * SHARE, SHARE), SHARE)
    out_ref[0] = x_own
    out_ref[1] = last_y[0, mine]
    out_ref[2] = primal_avg
    out_ref[3] = last_y[1, mine]
    for both, which in pending[:-1]:
        pltpu.make_async_copy(both, both, send_sems.at[which]).wait()
    fin_in()
    inner = jnp.sum(jnp.sum(fin_dst[...], axis=0), axis=1, keepdims=True)
    primal_scale = 1.0 / math.sqrt(n_cblocks * TILE * n_col)
    dual_scale = 1.0 / math.sqrt(n_rblocks * TILE * n_row)
    first = lax.broadcasted_iota(I32, (SHARE, TILE), 1) == 0
    out_ref[4] = jnp.where(first, inner[0:1] * primal_scale, inner[1:2] * dual_scale)
    both, which = pending[-1]
    pltpu.make_async_copy(both, both, send_sems.at[which]).wait()


def split_kernel(packed_ref, *out_refs):
    for i in range(4):
        out_refs[i][...] = packed_ref[i]
    out_refs[4][...] = packed_ref[4, 0:1, 0:2]


def solution(mesh):
    n_row, n_col = mesh.shape["row"], mesh.shape["col"]
    n_x, n_core = N_X, N_CORE
    n_z, n_y = n_row // n_x, n_col // n_core

    def body(
        tiles,
        tile_rows,
        tile_cols,
        tile_count,
        cost,
        upper,
        var_kind,
        rhs,
        row_kind,
        primal_start,
        dual_start,
    ):
        slots = tiles.shape[2]
        sizes = (n_x, n_z, n_y, n_core, slots)
        n_rblocks, n_cblocks = n_col * SHARE, n_row * SHARE
        n_last = n_row * n_core
        anywhere = pl.BlockSpec(memory_space=pl.ANY)
        vmem = pl.BlockSpec(memory_space=pltpu.VMEM)
        smem = pl.BlockSpec(memory_space=pltpu.SMEM)
        scratch = [
            ((slots, TILE, TILE), BF16),
            ((2, 1, slots), I32),
            ((3, n_cblocks, TILE), F32),
            ((n_cblocks, TILE), I32),
            ((2, n_rblocks, TILE), F32),
            ((n_rblocks, TILE), I32),
            ((2, TILE), I32),
            ((n_x, 2, TILE), I32),
            ((n_z, 2, TILE), I32),
            ((n_y, 2, TILE), I32),
            ((n_core, 2, TILE), I32),
            ((n_z * (slots + SHARE), n_x * TILE), BF16),
            ((n_y * (slots + SHARE), n_core * TILE), BF16),
            ((ITERS, 2 * slots, TILE), BF16),
            ((ITERS, n_x, 2 * slots, TILE), BF16),
            ((ITERS, n_z, slots, TILE), I16),
            ((ITERS, n_z, slots, TILE), I16),
            ((ITERS, n_z, 1, TILE), F32),
            ((ITERS, n_z, 1, TILE), F32),
            ((ITERS, n_z, SHARE, TILE), F32),
            ((ITERS, n_z, SHARE, TILE), F32),
            ((ITERS, 2 * slots, TILE), BF16),
            ((ITERS, n_core, 2 * slots, TILE), BF16),
            ((n_y, slots, TILE), I16),
            ((ITERS, n_y, slots, TILE), I16),
            ((n_y, 1, TILE), F32),
            ((ITERS, n_y, 1, TILE), F32),
            ((n_y, SHARE, TILE), F32),
            ((n_y, SHARE, TILE), F32),
            ((n_y * SHARE, TILE), I16),
            ((1, TILE), F32),
            ((SHARE, TILE), F32),
            ((n_y, SHARE, TILE), F32),
            ((1, TILE), F32),
            ((n_y, 1, TILE), F32),
            ((2, n_y * SHARE, TILE), F32),
            ((2, TILE), F32),
            ((n_last, 2, TILE), F32),
        ]
        packed = pl.pallas_call(
            functools.partial(kernel, sizes),
            out_shape=jax.ShapeDtypeStruct((5, SHARE, TILE), F32),
            in_specs=[anywhere] * 3 + [smem] + [anywhere] * 7,
            out_specs=vmem,
            scratch_shapes=[pltpu.VMEM(shape, dtype) for shape, dtype in scratch]
            + [
                pltpu.SemaphoreType.DMA((9 + slots // GROUP,)),
                pltpu.SemaphoreType.DMA((SEMS,)),
                pltpu.SemaphoreType.DMA((SEMS,)),
            ],
            compiler_params=pltpu.CompilerParams(
                collective_id=0, has_side_effects=True, vmem_limit_bytes=60 * 2**20
            ),
            name="pdhg",
        )(
            tiles.reshape(slots, TILE, TILE),
            tile_rows.reshape(1, slots),
            tile_cols.reshape(1, slots),
            tile_count,
            cost.reshape(n_cblocks, TILE),
            upper.reshape(n_cblocks, TILE),
            var_kind.reshape(n_cblocks, TILE),
            rhs.reshape(n_rblocks, TILE),
            row_kind.reshape(n_rblocks, TILE),
            primal_start.reshape(n_cblocks, TILE),
            dual_start.reshape(n_rblocks, TILE),
        )
        share = jax.ShapeDtypeStruct((SHARE, TILE), F32)
        outs = pl.pallas_call(
            split_kernel,
            out_shape=(share,) * 4 + (jax.ShapeDtypeStruct((1, 2), F32),),
            in_specs=[vmem],
            out_specs=(vmem,) * 5,
            name="unpack",
        )(packed)
        return tuple(o.reshape(-1) for o in outs)

    placed = (
        P("row", "col", None, None, None),
        P("row", "col", None),
        P("row", "col", None),
        P("row", "col"),
        P("col"),
        P("col"),
        P("col"),
        P("row"),
        P("row"),
        P("col"),
        P("row"),
    )
    return jax.shard_map(
        body,
        mesh=mesh,
        in_specs=placed,
        out_specs=(P(("col", "row")), P(("row", "col")), P(("col", "row")), P(("row", "col")), P()),
        check_vma=False,
    )
```

time: 70.6 us -> 67.2 us (0.952)
  Pallas kernels: 67.8 us -> 65.7 us
  local copies, waits for them, and re-layouts: 1.19 us -> 0 us
    pallas_call x1, Pallas kernels: 66.5 us -> 64.4 us  [body(): pl.pallas_call(functools.partial(kernel, sizes), out_shape=jax.ShapeDtype...]
    squeeze x1 -> x0, local copies, waits for them, and re-layouts: 1.19 us -> none  [body(): return tuple((o.reshape(-1) for o in outs[:4])) + (outs[4][0, :2],)]
where the time goes in v2:
time: 67.2 us; the launch traced here: 67 us
  Pallas kernels  65.7 us (98%)
  between operations  1.29 us (2%)
    pallas_call x1, Pallas kernels, body(): pl.pallas_call(functools.partial(kernel, sizes), out_shape=jax.ShapeDtype...  64.4 us

profile of v2, /device:TPU:1, one launch (start us, length us, event | category | flops | bytes accessed | tf_op | source)
XLA Modules:
  0.0 67.0 jit_solution(4258834825534646039)
XLA Ops:
  1.3 64.4 %pdhg.1.packed_ref = f32[5,8,128]{2,1,0:T(8,128)} custom-call(bf16[64,128,128]{2,1,0:T(8,128)(2,1)} %bitcast.15, s32[1,64]{1,0:T(1,128)} %bitcast.23, s32[1,64]{1,0:T(1,128)} %bitcast.24, s32[1,1]{1,0:T(1,128)S(6)} %copy.16.count_ref, f32[256,128]{1,0:T(8,128)} %bitcast.16, f32[256,128]{1,0:T(8,128)} %bitcast.17, s32[256,128]{1,0:T(8,128)} %bitcast.18, ...), custom_call_target="tpu_custom_call" | custom-call | tf_op jit(solution)/shard_map/pdhg/pallas_call | solution.py:509
  65.7 1.3 %unpack.1 = (f32[8,128]{1,0:T(8,128)}, f32[8,128]{1,0:T(8,128)}, f32[8,128]{1,0:T(8,128)}, f32[8,128]{1,0:T(8,128)}, f32[1,2]{1,0:T(1,128)}) custom-call(f32[5,8,128]{2,1,0:T(8,128)} %pdhg.1.packed_ref), custom_call_target="tpu_custom_call" | custom-call | tf_op jit(solution)/shard_map/unpack/pallas_call | solution.py:538

commit v3 on v2

--- a/solution.py
+++ b/solution.py
@@ -45,10 +45,13 @@
     return jnp.where(lane < TILE // 2, wide, pltpu.roll(wide, TILE // 2, 1))
 
 
-def quantize(sums):
-    top = jnp.max(jnp.abs(sums), axis=-2, keepdims=True)
+def lane_top(sums):
+    return jnp.max(jnp.abs(sums), axis=-2, keepdims=True)
+
+
+def levels_of(sums, top):
     inverse = LEVELS / jnp.maximum(top, 1e-30)
-    return jnp.round(sums * inverse).astype(I32).astype(I16), top * (1.0 / LEVELS)
+    return jnp.round(sums * inverse).astype(I32).astype(I16)
 
 
 def kernel(
@@ -138,17 +141,7 @@
         at_core = lax.rem(my_core + n_core - 1 - lax.rem(step, n_core), n_core)
         return step, (at_x * n_z + at_z, my_y * n_core + at_core)
 
-    barrier = pltpu.get_barrier_semaphore()
     n_last = n_row * n_core
-
-    @pl.loop(0, n_last - 1)
-    def _(step):
-        pl.semaphore_signal(barrier, inc=1, device_id=last_peer(step)[1], device_id_type=MESH)
-
-    @pl.loop(0, n_y - 1)
-    def _(step):
-        pl.semaphore_signal(barrier, inc=1, device_id=y_peer(step)[1], device_id_type=MESH)
-
     n_groups = slots // GROUP
     pieces = [pl.ds(g * GROUP, GROUP) for g in range(n_groups)]
     first_loads = [
@@ -171,6 +164,15 @@
     ]
     for copy in copies:
         copy.start()
+    barrier = pltpu.get_barrier_semaphore()
+
+    greeted = ((z_peer, n_z - 1), (y_peer, n_y - 1), (x_peer, n_x - 1), (core_peer, n_core - 1))
+    for peer, count in greeted:
+
+        @pl.loop(0, count)
+        def _(step):
+            pl.semaphore_signal(barrier, inc=1, device_id=peer(step)[1], device_id_type=MESH)
+
     n_first, n_tile = len(first_loads), len(tile_loads)
     for copy in copies[:n_first]:
         copy.wait()
@@ -247,7 +249,7 @@
     idx_src[...] = jnp.full((2, TILE), -1, I32)
     idx_src[0:1, 0:slots] = block_cols
     idx_src[1:2, 0:slots] = block_rows
-    pl.semaphore_wait(barrier, n_last - 1 + n_y - 1)
+    pl.semaphore_wait(barrier, sum(count for _, count in greeted))
 
     z_idx_in = send(z_peer, n_z - 1, lambda at: idx_src, idx_z, my_z)
     x_idx_in = send(x_peer, n_x - 1, lambda at: idx_src, idx_x, my_x)
@@ -327,11 +329,15 @@
             px_dst[it].reshape(n_x * 2 * slots, TILE),
             preferred_element_type=F32,
         )
-        zq_src[it], zs_src[it] = quantize(sums[:n_zneed].reshape(n_z, slots, TILE))
+        wanted = sums[:n_zneed].reshape(n_z, slots, TILE)
+        top = lane_top(wanted)
+        zs_src[it] = top * (1.0 / LEVELS)
+        zs_in = send(z_peer, n_z - 1, lambda at: zs_src.at[it, at], zs_dst.at[it], my_z)
+        zq_src[it] = levels_of(wanted, top)
         zq_in = send(z_peer, n_z - 1, lambda at: zq_src.at[it, at], zq_dst.at[it], my_z)
-        zs_in = send(z_peer, n_z - 1, lambda at: zs_src.at[it, at], zs_dst.at[it], my_z)
         zo_src[it] = sums[n_zneed:].reshape(n_z, SHARE, TILE)
-        zo_in = send(z_peer, n_z - 1, lambda at: zo_src.at[it, at], zo_dst.at[it], my_z)
+        if last:
+            zo_in = send(z_peer, n_z - 1, lambda at: zo_src.at[it, at], zo_dst.at[it], my_z)
         zq_dst[it, my_z] = zq_src[it, my_z]
         zs_dst[it, my_z] = zs_src[it, my_z]
         zo_dst[it, my_z] = zo_src[it, my_z]
@@ -350,29 +356,40 @@
             kind_need,
             upper_need,
         )
+        if not last:
+            zo_in = send(z_peer, n_z - 1, lambda at: zo_src.at[it, at], zo_dst.at[it], my_z)
         put_split(pc_src.at[it], fore((2.0 * x_new - x_need).astype(BF16)))
         x_need = x_new
         c_in = send(core_peer, n_core - 1, lambda at: pc_src.at[it], pc_dst.at[it], my_core)
         pc_dst[it, my_core] = pc_src[it]
-        zo_in()
-        x_own = project_primal(
-            x_own - PRIMAL_STEP * (cost_own - jnp.sum(zo_dst[it], axis=0)), kind_own, upper_own
-        )
-        x_total = x_total + x_own
+        if last:
+            zo_in()
+            x_own = project_primal(
+                x_own - PRIMAL_STEP * (cost_own - jnp.sum(zo_dst[it], axis=0)), kind_own, upper_own
+            )
+            x_total = x_total + x_own
         c_in()
         parts = pc_dst[it].reshape(n_core * 2 * slots, TILE)
         if not last:
             sums = jnp.dot(match_y[...], parts, preferred_element_type=F32)
-            yq_src[...], ys_src[...] = quantize(sums[:n_yneed].reshape(n_y, slots, TILE))
+            wanted = sums[:n_yneed].reshape(n_y, slots, TILE)
+            top = lane_top(wanted)
+            ys_src[...] = top * (1.0 / LEVELS)
+            ys_in = send(y_peer, n_y - 1, lambda at: ys_src.at[at], ys_dst.at[it], my_y)
+            yq_src[...] = levels_of(wanted, top)
             yq_in = send(y_peer, n_y - 1, lambda at: yq_src.at[at], yq_dst.at[it], my_y)
-            ys_in = send(y_peer, n_y - 1, lambda at: ys_src.at[at], ys_dst.at[it], my_y)
             yo_src[...] = sums[n_yneed:].reshape(n_y, SHARE, TILE)
-            yo_in = send(y_peer, n_y - 1, lambda at: yo_src.at[at], yo_dst, my_y)
             yq_dst[it, my_y] = yq_src[my_y]
             ys_dst[it, my_y] = ys_src[my_y]
             yo_dst[my_y] = yo_src[my_y]
+            zo_in()
+            x_own = project_primal(
+                x_own - PRIMAL_STEP * (cost_own - jnp.sum(zo_dst[it], axis=0)), kind_own, upper_own
+            )
+            x_total = x_total + x_own
             yq_in()
             ys_in()
+            yo_in = send(y_peer, n_y - 1, lambda at: yo_src.at[at], yo_dst, my_y)
             y_need = project_dual(
                 y_need + DUAL_STEP * (rhs_need - total(yq_dst[it], ys_dst[it])), rkind_need
             )
@@ -383,9 +400,11 @@
             px_dst[it + 1, my_x] = px_src[it + 1]
 
     sums = jnp.dot(match_y[n_yneed:], parts, preferred_element_type=F32)
-    lq_src[...], ls_src[...] = quantize(sums)
+    top = lane_top(sums)
+    ls_src[...] = top * (1.0 / LEVELS)
+    ys_in = send(y_peer, n_y - 1, lambda at: ls_src, ys_dst.at[ITERS - 1], my_y)
+    lq_src[...] = levels_of(sums, top)
     yq_in = send(y_peer, n_y - 1, lambda at: lq_src, yq_dst.at[ITERS - 1], my_y)
-    ys_in = send(y_peer, n_y - 1, lambda at: ls_src, ys_dst.at[ITERS - 1], my_y)
     primal_avg = x_total / ITERS
     po_src[...] = jnp.sum(cost_own * primal_avg, axis=0, keepdims=True)
     po_in = send(y_peer, n_y - 1, lambda at: po_src, po_dst, my_y)

time: 67.2 us -> 62.4 us (0.929)
  Pallas kernels: 65.7 us -> 60.9 us
    pallas_call x1, Pallas kernels: 64.4 us -> 59.6 us  [body(): pl.pallas_call(functools.partial(kernel, sizes), out_shape=jax.ShapeDtype...]
where the time goes in v3:
time: 62.4 us; the launch traced here: 62.2 us
  Pallas kernels  60.9 us (98%)
  between operations  1.29 us (2%)
    pallas_call x1, Pallas kernels, body(): pl.pallas_call(functools.partial(kernel, sizes), out_shape=jax.ShapeDtype...  59.6 us
    pallas_call x1, Pallas kernels, body(): pl.pallas_call(split_kernel, out_shape=(share,) * 4 + (jax.ShapeDtypeStru...  1.34 us

profile of v3, /device:TPU:1, one launch (start us, length us, event | category | flops | bytes accessed | tf_op | source)
XLA Modules:
  0.0 62.2 jit_solution(602808083917865537)
XLA Ops:
  1.3 59.6 %pdhg.1.packed_ref = f32[5,8,128]{2,1,0:T(8,128)} custom-call(bf16[64,128,128]{2,1,0:T(8,128)(2,1)} %bitcast.15, s32[1,64]{1,0:T(1,128)} %bitcast.23, s32[1,64]{1,0:T(1,128)} %bitcast.24, s32[1,1]{1,0:T(1,128)S(6)} %copy.16.count_ref, f32[256,128]{1,0:T(8,128)} %bitcast.16, f32[256,128]{1,0:T(8,128)} %bitcast.17, s32[256,128]{1,0:T(8,128)} %bitcast.18, ...), custom_call_target="tpu_custom_call" | custom-call | tf_op jit(solution)/shard_map/pdhg/pallas_call | solution.py:528
  60.9 1.3 %unpack.1 = (f32[8,128]{1,0:T(8,128)}, f32[8,128]{1,0:T(8,128)}, f32[8,128]{1,0:T(8,128)}, f32[8,128]{1,0:T(8,128)}, f32[1,2]{1,0:T(1,128)}) custom-call(f32[5,8,128]{2,1,0:T(8,128)} %pdhg.1.packed_ref), custom_call_target="tpu_custom_call" | custom-call | tf_op jit(solution)/shard_map/unpack/pallas_call | solution.py:557

commit v4 on v3

--- a/solution.py
+++ b/solution.py
@@ -69,6 +69,7 @@
     dual_hbm,
     out_ref,
     tiles,
+    turned,
     raw_idx,
     col_vecs,
     col_kind,
@@ -185,56 +186,54 @@
     )
     sub = lax.broadcasted_iota(I32, (GROUP, TILE), 0)
 
+    def spread(part):
+        return jnp.concatenate(
+            [jnp.where(sub == j, part, 0.0).astype(BF16) for j in range(GROUP)], axis=1
+        )
+
     def back(part_of, ready):
         products = []
         for g in range(n_groups):
             ready(g)
             part = part_of[g * GROUP : (g + 1) * GROUP]
-            spread = jnp.concatenate(
-                [jnp.where(sub == j, part, 0.0).astype(BF16) for j in range(GROUP)], axis=1
-            )
             block = tiles[g * GROUP : (g + 1) * GROUP].reshape(GROUP * TILE, TILE)
-            products.append(jnp.dot(spread, block, preferred_element_type=F32))
+            products.append(jnp.dot(spread(part), block, preferred_element_type=F32))
         return jnp.concatenate(products, axis=0)
 
     def fore(part_of):
         products = []
         for g in range(n_groups):
             part = part_of[g * GROUP : (g + 1) * GROUP]
-            block = tiles[g * GROUP : (g + 1) * GROUP].reshape(GROUP * TILE, TILE)
-            every = lax.dot_general(
-                part, block, (((1,), (1,)), ((), ())), preferred_element_type=F32
-            )
-            own = jnp.zeros((GROUP, TILE), F32)
-            for j in range(GROUP):
-                own = own + jnp.where(sub == j, every[:, j * TILE : (j + 1) * TILE], 0.0)
-            products.append(own)
+            block = turned[g * GROUP : (g + 1) * GROUP].reshape(GROUP * TILE, TILE)
+            products.append(jnp.dot(spread(part), block, preferred_element_type=F32))
         return jnp.concatenate(products, axis=0)
 
     pending = []
     used = [0]
 
-    def send(peer, count, source, dest, slot):
-        sem = used[0]
-        used[0] += 1
+    def send(peer, count, slot, *pairs):
+        base = used[0]
+        used[0] += len(pairs)
 
         @pl.loop(0, count)
         def _(step):
             at, device = peer(step)
-            pltpu.make_async_remote_copy(
-                src_ref=source(at),
-                dst_ref=dest.at[slot],
-                send_sem=send_sems.at[sem],
-                recv_sem=recv_sems.at[sem],
-                device_id=device,
-                device_id_type=MESH,
-            ).start()
-
-        both = dest.at[pl.ds(0, count)]
-        pending.append((both, sem))
+            for k, (source, dest) in enumerate(pairs):
+                pltpu.make_async_remote_copy(
+                    src_ref=source(at),
+                    dst_ref=dest.at[slot],
+                    send_sem=send_sems.at[base + k],
+                    recv_sem=recv_sems.at[base + k],
+                    device_id=device,
+                    device_id_type=MESH,
+                ).start()
+
+        started = [(dest.at[pl.ds(0, count)], base + k) for k, (_, dest) in enumerate(pairs)]
+        pending.extend(started)
 
         def arrive():
-            pltpu.make_async_copy(both, both, recv_sems.at[sem]).wait()
+            for both, sem in started:
+                pltpu.make_async_copy(both, both, recv_sems.at[sem]).wait()
 
         return arrive
 
@@ -251,11 +250,11 @@
     idx_src[1:2, 0:slots] = block_rows
     pl.semaphore_wait(barrier, sum(count for _, count in greeted))
 
-    z_idx_in = send(z_peer, n_z - 1, lambda at: idx_src, idx_z, my_z)
-    x_idx_in = send(x_peer, n_x - 1, lambda at: idx_src, idx_x, my_x)
-    x_in = send(x_peer, n_x - 1, lambda at: px_src.at[0], px_dst.at[0], my_x)
-    y_idx_in = send(y_peer, n_y - 1, lambda at: idx_src, idx_y, my_y)
-    c_idx_in = send(core_peer, n_core - 1, lambda at: idx_src, idx_c, my_core)
+    z_idx_in = send(z_peer, n_z - 1, my_z, (lambda at: idx_src, idx_z))
+    x_idx_in = send(x_peer, n_x - 1, my_x, (lambda at: idx_src, idx_x))
+    x_in = send(x_peer, n_x - 1, my_x, (lambda at: px_src.at[0], px_dst.at[0]))
+    y_idx_in = send(y_peer, n_y - 1, my_y, (lambda at: idx_src, idx_y))
+    c_idx_in = send(core_peer, n_core - 1, my_core, (lambda at: idx_src, idx_c))
     for mine, ref in ((my_x, idx_x), (my_z, idx_z), (my_y, idx_y), (my_core, idx_c)):
         ref[mine] = idx_src[...]
     px_dst[0, my_x] = px_src[0]
@@ -274,13 +273,6 @@
     x_need, cost_need, upper_need, kind_need = (
         col_got[:, i * TILE : (i + 1) * TILE] for i in range(4)
     )
-    row_all = jnp.concatenate(
-        [row_vecs[0], row_vecs[1], row_kind_full[...].astype(F32)], axis=1
-    )
-    row_got = jnp.dot(
-        row_pick, row_all, precision=lax.Precision.HIGHEST, preferred_element_type=F32
-    )
-    y_need, rhs_need, rkind_need = (row_got[:, i * TILE : (i + 1) * TILE] for i in range(3))
     row_share = pl.ds(pl.multiple_of(me_row * SHARE, SHARE), SHARE)
     col_share = pl.ds(pl.multiple_of(me_col * SHARE, SHARE), SHARE)
     x_own, cost_own, upper_own = (col_vecs[i, row_share] for i in range(3))
@@ -300,21 +292,6 @@
                 need_cols[:, z : z + 1] == have_wide, 1.0, 0.0
             ).astype(BF16)
         match_z[n_z * slots :, lanes] = jnp.where(own_cols == have[0:1], 1.0, 0.0).astype(BF16)
-    y_idx_in()
-    c_idx_in()
-    need_rows = idx_y[:, 1, :].astype(F32).T[:slots]
-    own_at = lax.broadcasted_iota(I32, (n_y * SHARE, TILE), 0)
-    own_rows = (lax.div(own_at, SHARE) * n_core + my_core) * SHARE + lax.rem(own_at, SHARE)
-    for k in range(n_core):
-        have = twice(idx_c[k, 1:2])
-        lanes = slice(k * TILE, (k + 1) * TILE)
-        have_wide = jnp.broadcast_to(have[0:1], (slots, TILE)).astype(F32)
-        for y in range(n_y):
-            match_y[y * slots : (y + 1) * slots, lanes] = jnp.where(
-                need_rows[:, y : y + 1] == have_wide, 1.0, 0.0
-            ).astype(BF16)
-        match_y[n_y * slots :, lanes] = jnp.where(own_rows == have[0:1], 1.0, 0.0).astype(BF16)
-
     def total(levels, scales):
         return jnp.sum(levels.astype(F32) * scales, axis=0)
 
@@ -332,12 +309,17 @@
         wanted = sums[:n_zneed].reshape(n_z, slots, TILE)
         top = lane_top(wanted)
         zs_src[it] = top * (1.0 / LEVELS)
-        zs_in = send(z_peer, n_z - 1, lambda at: zs_src.at[it, at], zs_dst.at[it], my_z)
         zq_src[it] = levels_of(wanted, top)
-        zq_in = send(z_peer, n_z - 1, lambda at: zq_src.at[it, at], zq_dst.at[it], my_z)
+        zq_in = send(
+            z_peer,
+            n_z - 1,
+            my_z,
+            (lambda at: zs_src.at[it, at], zs_dst.at[it]),
+            (lambda at: zq_src.at[it, at], zq_dst.at[it]),
+        )
         zo_src[it] = sums[n_zneed:].reshape(n_z, SHARE, TILE)
         if last:
-            zo_in = send(z_peer, n_z - 1, lambda at: zo_src.at[it, at], zo_dst.at[it], my_z)
+            zo_in = send(z_peer, n_z - 1, my_z, (lambda at: zo_src.at[it, at], zo_dst.at[it]))
         zq_dst[it, my_z] = zq_src[it, my_z]
         zs_dst[it, my_z] = zs_src[it, my_z]
         zo_dst[it, my_z] = zo_src[it, my_z]
@@ -347,20 +329,47 @@
                 y_own + DUAL_STEP * (rhs_own - jnp.sum(yo_dst[...], axis=0)), rkind_own
             )
             mid_src[...] = y_first
-            mid_in = send(y_peer, n_y - 1, lambda at: mid_src, mid_dst, my_y)
+            mid_in = send(y_peer, n_y - 1, my_y, (lambda at: mid_src, mid_dst))
             mid_dst[my_y] = y_first
+        if it == 0:
+            row_all = jnp.concatenate(
+                [row_vecs[0], row_vecs[1], row_kind_full[...].astype(F32)], axis=1
+            )
+            row_got = jnp.dot(
+                row_pick, row_all, precision=lax.Precision.HIGHEST, preferred_element_type=F32
+            )
+            y_need, rhs_need, rkind_need = (row_got[:, i * TILE : (i + 1) * TILE] for i in range(3))
+            y_idx_in()
+            c_idx_in()
+            need_rows = idx_y[:, 1, :].astype(F32).T[:slots]
+            own_at = lax.broadcasted_iota(I32, (n_y * SHARE, TILE), 0)
+            own_rows = (lax.div(own_at, SHARE) * n_core + my_core) * SHARE + lax.rem(own_at, SHARE)
+            for k in range(n_core):
+                have = twice(idx_c[k, 1:2])
+                lanes = slice(k * TILE, (k + 1) * TILE)
+                have_wide = jnp.broadcast_to(have[0:1], (slots, TILE)).astype(F32)
+                for y in range(n_y):
+                    match_y[y * slots : (y + 1) * slots, lanes] = jnp.where(
+                        need_rows[:, y : y + 1] == have_wide, 1.0, 0.0
+                    ).astype(BF16)
+                match_y[n_y * slots :, lanes] = jnp.where(own_rows == have[0:1], 1.0, 0.0).astype(BF16)
+
+            @pl.loop(0, slots // 8)
+            def _(part):
+                for k in range(8):
+                    turned[part * 8 + k] = tiles[part * 8 + k].T
+
         zq_in()
-        zs_in()
         x_new = project_primal(
             x_need - PRIMAL_STEP * (cost_need - total(zq_dst[it], zs_dst[it])),
             kind_need,
             upper_need,
         )
         if not last:
-            zo_in = send(z_peer, n_z - 1, lambda at: zo_src.at[it, at], zo_dst.at[it], my_z)
-        put_split(pc_src.at[it], fore((2.0 * x_new - x_need).astype(BF16)))
+            zo_in = send(z_peer, n_z - 1, my_z, (lambda at: zo_src.at[it, at], zo_dst.at[it]))
+        put_split(pc_src.at[it], fore((2.0 * x_new - x_need).astype(BF16).astype(F32)))
         x_need = x_new
-        c_in = send(core_peer, n_core - 1, lambda at: pc_src.at[it], pc_dst.at[it], my_core)
+        c_in = send(core_peer, n_core - 1, my_core, (lambda at: pc_src.at[it], pc_dst.at[it]))
         pc_dst[it, my_core] = pc_src[it]
         if last:
             zo_in()
@@ -375,9 +384,14 @@
             wanted = sums[:n_yneed].reshape(n_y, slots, TILE)
             top = lane_top(wanted)
             ys_src[...] = top * (1.0 / LEVELS)
-            ys_in = send(y_peer, n_y - 1, lambda at: ys_src.at[at], ys_dst.at[it], my_y)
             yq_src[...] = levels_of(wanted, top)
-            yq_in = send(y_peer, n_y - 1, lambda at: yq_src.at[at], yq_dst.at[it], my_y)
+            yq_in = send(
+                y_peer,
+                n_y - 1,
+                my_y,
+                (lambda at: ys_src.at[at], ys_dst.at[it]),
+                (lambda at: yq_src.at[at], yq_dst.at[it]),
+            )
             yo_src[...] = sums[n_yneed:].reshape(n_y, SHARE, TILE)
             yq_dst[it, my_y] = yq_src[my_y]
             ys_dst[it, my_y] = ys_src[my_y]
@@ -388,26 +402,30 @@
             )
             x_total = x_total + x_own
             yq_in()
-            ys_in()
-            yo_in = send(y_peer, n_y - 1, lambda at: yo_src.at[at], yo_dst, my_y)
+            yo_in = send(y_peer, n_y - 1, my_y, (lambda at: yo_src.at[at], yo_dst))
             y_need = project_dual(
                 y_need + DUAL_STEP * (rhs_need - total(yq_dst[it], ys_dst[it])), rkind_need
             )
             put_split(
                 px_src.at[it + 1], back(y_need.astype(BF16).astype(F32), lambda g: None)
             )
-            x_in = send(x_peer, n_x - 1, lambda at: px_src.at[it + 1], px_dst.at[it + 1], my_x)
+            x_in = send(x_peer, n_x - 1, my_x, (lambda at: px_src.at[it + 1], px_dst.at[it + 1]))
             px_dst[it + 1, my_x] = px_src[it + 1]
 
     sums = jnp.dot(match_y[n_yneed:], parts, preferred_element_type=F32)
     top = lane_top(sums)
     ls_src[...] = top * (1.0 / LEVELS)
-    ys_in = send(y_peer, n_y - 1, lambda at: ls_src, ys_dst.at[ITERS - 1], my_y)
     lq_src[...] = levels_of(sums, top)
-    yq_in = send(y_peer, n_y - 1, lambda at: lq_src, yq_dst.at[ITERS - 1], my_y)
+    yq_in = send(
+        y_peer,
+        n_y - 1,
+        my_y,
+        (lambda at: ls_src, ys_dst.at[ITERS - 1]),
+        (lambda at: lq_src, yq_dst.at[ITERS - 1]),
+    )
     primal_avg = x_total / ITERS
     po_src[...] = jnp.sum(cost_own * primal_avg, axis=0, keepdims=True)
-    po_in = send(y_peer, n_y - 1, lambda at: po_src, po_dst, my_y)
+    po_in = send(y_peer, n_y - 1, my_y, (lambda at: po_src, po_dst))
     yq_dst[ITERS - 1, my_y] = lq_src[...]
     ys_dst[ITERS - 1, my_y] = ls_src[...]
     po_dst[my_y] = po_src[...]
@@ -426,14 +444,13 @@
     po_in()
     fin_src[0:1] = jnp.sum(po_dst[...], axis=0)
     yq_in()
-    ys_in()
     half_new = project_dual(
         half_y + DUAL_STEP * (half_rhs - total(yq_dst[ITERS - 1], ys_dst[ITERS - 1])), half_kind
     )
     half_avg = (half_y + half_new) / ITERS
     fin_src[1:2] = jnp.sum(half_rhs * half_avg, axis=0, keepdims=True)
     me_last = me_row * n_core + my_core
-    fin_in = send(last_peer, n_last - 1, lambda at: fin_src, fin_dst, me_last)
+    fin_in = send(last_peer, n_last - 1, me_last, (lambda at: fin_src, fin_dst))
     fin_dst[me_last] = fin_src[...]
     last_y[0] = half_new
     last_y[1] = half_avg
@@ -486,6 +503,7 @@
         vmem = pl.BlockSpec(memory_space=pltpu.VMEM)
         smem = pl.BlockSpec(memory_space=pltpu.SMEM)
         scratch = [
+            ((slots, TILE, TILE), BF16),
             ((slots, TILE, TILE), BF16),
             ((2, 1, slots), I32),
             ((3, n_cblocks, TILE), F32),
@@ -525,9 +543,12 @@
             ((2, TILE), F32),
             ((n_last, 2, TILE), F32),
         ]
+        def in_hbm(array):
+            return pltpu.with_memory_space_constraint(array, pltpu.HBM)
+
         packed = pl.pallas_call(
             functools.partial(kernel, sizes),
-            out_shape=jax.ShapeDtypeStruct((5, SHARE, TILE), F32),
+            out_shape=pltpu.VMEM((5, SHARE, TILE), F32),
             in_specs=[anywhere] * 3 + [smem] + [anywhere] * 7,
             out_specs=vmem,
             scratch_shapes=[pltpu.VMEM(shape, dtype) for shape, dtype in scratch]
@@ -537,21 +558,21 @@
                 pltpu.SemaphoreType.DMA((SEMS,)),
             ],
             compiler_params=pltpu.CompilerParams(
-                collective_id=0, has_side_effects=True, vmem_limit_bytes=60 * 2**20
+                collective_id=0, has_side_effects=True, vmem_limit_bytes=48 * 2**20
             ),
             name="pdhg",
         )(
-            tiles.reshape(slots, TILE, TILE),
-            tile_rows.reshape(1, slots),
-            tile_cols.reshape(1, slots),
+            in_hbm(tiles.reshape(slots, TILE, TILE)),
+            in_hbm(tile_rows.reshape(1, slots)),
+            in_hbm(tile_cols.reshape(1, slots)),
             tile_count,
-            cost.reshape(n_cblocks, TILE),
-            upper.reshape(n_cblocks, TILE),
-            var_kind.reshape(n_cblocks, TILE),
-            rhs.reshape(n_rblocks, TILE),
-            row_kind.reshape(n_rblocks, TILE),
-            primal_start.reshape(n_cblocks, TILE),
-            dual_start.reshape(n_rblocks, TILE),
+            in_hbm(cost.reshape(n_cblocks, TILE)),
+            in_hbm(upper.reshape(n_cblocks, TILE)),
+            in_hbm(var_kind.reshape(n_cblocks, TILE)),
+            in_hbm(rhs.reshape(n_rblocks, TILE)),
+            in_hbm(row_kind.reshape(n_rblocks, TILE)),
+            in_hbm(primal_start.reshape(n_cblocks, TILE)),
+            in_hbm(dual_start.reshape(n_rblocks, TILE)),
         )
         share = jax.ShapeDtypeStruct((SHARE, TILE), F32)
         outs = pl.pallas_call(
@@ -560,7 +581,7 @@
             in_specs=[vmem],
             out_specs=(vmem,) * 5,
             name="unpack",
-        )(packed)
+        )(pltpu.with_memory_space_constraint(packed, pltpu.VMEM))
         return tuple(o.reshape(-1) for o in outs)
 
     placed = (

time: 62.4 us -> 59.7 us (0.957)
  Pallas kernels: 60.9 us -> 58.2 us
    pallas_call x1, Pallas kernels: 59.6 us -> 57.6 us  [body(): pl.pallas_call(functools.partial(kernel, sizes), out_shape=pltpu.VMEM((5,...]
    pallas_call x1, Pallas kernels: 1.34 us -> 0.61 us  [body(): pl.pallas_call(split_kernel, out_shape=(share,) * 4 + (jax.ShapeDtypeStru...]
where the time goes in v4:
time: 59.7 us; the launch traced here: 59.5 us
  Pallas kernels  58.2 us (97%)
  between operations  1.29 us (2%)
    pallas_call x1, Pallas kernels, body(): pl.pallas_call(functools.partial(kernel, sizes), out_shape=pltpu.VMEM((5,...  57.6 us

profile of v4, /device:TPU:1, one launch (start us, length us, event | category | flops | bytes accessed | tf_op | source)
XLA Modules:
  0.0 59.5 jit_solution(10979610531990419088)
XLA Ops:
  1.3 57.6 %pdhg.1.packed_ref = f32[5,8,128]{2,1,0:T(8,128)S(1)} custom-call(bf16[64,128,128]{2,1,0:T(8,128)(2,1)} %bitcast.15, s32[1,64]{1,0:T(1,128)} %bitcast.23, s32[1,64]{1,0:T(1,128)} %bitcast.24, s32[1,1]{1,0:T(1,128)S(6)} %copy.16.count_ref, f32[256,128]{1,0:T(8,128)} %bitcast.16, f32[256,128]{1,0:T(8,128)} %bitcast.17, s32[256,128]{1,0:T(8,128)} %bitcast.18, ...), custom_call_target="tpu_custom_call" | custom-call | tf_op jit(solution)/shard_map/pdhg/pallas_call | solution.py:549
  58.9 0.6 %unpack.1 = (f32[8,128]{1,0:T(8,128)}, f32[8,128]{1,0:T(8,128)}, f32[8,128]{1,0:T(8,128)}, f32[8,128]{1,0:T(8,128)}, f32[1,2]{1,0:T(1,128)}) custom-call(f32[5,8,128]{2,1,0:T(8,128)S(1)} %pdhg.1.packed_ref), custom_call_target="tpu_custom_call" | custom-call | tf_op jit(solution)/shard_map/unpack/pallas_call | solution.py:578

commit v5 on v4

--- a/solution.py
+++ b/solution.py
@@ -23,6 +23,7 @@
 I32 = jnp.int32
 I16 = jnp.int16
 SEMS = 24
+CHUNKS = 2
 
 
 def project_primal(value, var_kind, upper):
@@ -35,8 +36,15 @@
 
 
 def zigzag(step, size):
+    if isinstance(step, int):
+        return size // 2 + (step + 1) // 2 * (1 - 2 * (step % 2))
     half = lax.div(step + 1, 2)
     return size // 2 + jnp.where(lax.rem(step, 2) == 0, half, -half)
+
+
+def backward(size):
+    ahead = [zigzag(step, size) % size for step in range(size)]
+    return [ahead.index((size - offset) % size) for offset in ahead]
 
 
 def twice(row):
@@ -136,11 +144,11 @@
         return at, (me_row, my_y * n_core + at)
 
     def last_peer(step):
-        ahead = lax.div(step, n_core)
-        at_z = lax.rem(my_z + zigzag(lax.div(ahead, n_x), n_z), n_z)
-        at_x = lax.rem(my_x + zigzag(lax.rem(ahead, n_x), n_x), n_x)
-        at_core = lax.rem(my_core + n_core - 1 - lax.rem(step, n_core), n_core)
-        return step, (at_x * n_z + at_z, my_y * n_core + at_core)
+        ahead = step // n_core
+        to_z = lax.rem(my_z + zigzag(ahead // n_x, n_z), n_z)
+        to_x = lax.rem(my_x + zigzag(ahead % n_x, n_x), n_x)
+        to_core = lax.rem(my_core + n_core - 1 - step % n_core, n_core)
+        return step, (to_x * n_z + to_z, my_y * n_core + to_core)
 
     n_last = n_row * n_core
     n_groups = slots // GROUP
@@ -211,22 +219,22 @@
     pending = []
     used = [0]
 
-    def send(peer, count, slot, *pairs):
+    def channel(peer, count, slot, *pairs):
         base = used[0]
         used[0] += len(pairs)
 
-        @pl.loop(0, count)
-        def _(step):
-            at, device = peer(step)
-            for k, (source, dest) in enumerate(pairs):
-                pltpu.make_async_remote_copy(
-                    src_ref=source(at),
-                    dst_ref=dest.at[slot],
-                    send_sem=send_sems.at[base + k],
-                    recv_sem=recv_sems.at[base + k],
-                    device_id=device,
-                    device_id_type=MESH,
-                ).start()
+        def start(low, high):
+            for step in range(low, high):
+                device = peer(step)[1]
+                for k, (source, dest) in enumerate(pairs):
+                    pltpu.make_async_remote_copy(
+                        src_ref=source(step),
+                        dst_ref=dest.at[slot(step)],
+                        send_sem=send_sems.at[base + k],
+                        recv_sem=recv_sems.at[base + k],
+                        device_id=device,
+                        device_id_type=MESH,
+                    ).start()
 
         started = [(dest.at[pl.ds(0, count)], base + k) for k, (_, dest) in enumerate(pairs)]
         pending.extend(started)
@@ -235,7 +243,27 @@
             for both, sem in started:
                 pltpu.make_async_copy(both, both, recv_sems.at[sem]).wait()
 
+        return start, arrive
+
+    def send(peer, count, slot, *pairs):
+        start, arrive = channel(peer, count, slot, *pairs)
+        start(0, count)
         return arrive
+
+    def z_slot(step):
+        return backward(n_z)[step]
+
+    def y_slot(step):
+        return backward(n_y)[step]
+
+    def at_x(step):
+        return my_x
+
+    def at_y(step):
+        return my_y
+
+    def at_core(step):
+        return my_core
 
     def put_split(ref, products):
         high = products.astype(BF16)
@@ -250,12 +278,12 @@
     idx_src[1:2, 0:slots] = block_rows
     pl.semaphore_wait(barrier, sum(count for _, count in greeted))
 
-    z_idx_in = send(z_peer, n_z - 1, my_z, (lambda at: idx_src, idx_z))
-    x_idx_in = send(x_peer, n_x - 1, my_x, (lambda at: idx_src, idx_x))
-    x_in = send(x_peer, n_x - 1, my_x, (lambda at: px_src.at[0], px_dst.at[0]))
-    y_idx_in = send(y_peer, n_y - 1, my_y, (lambda at: idx_src, idx_y))
-    c_idx_in = send(core_peer, n_core - 1, my_core, (lambda at: idx_src, idx_c))
-    for mine, ref in ((my_x, idx_x), (my_z, idx_z), (my_y, idx_y), (my_core, idx_c)):
+    z_idx_in = send(z_peer, n_z - 1, z_slot, (lambda step: idx_src, idx_z))
+    x_idx_in = send(x_peer, n_x - 1, at_x, (lambda step: idx_src, idx_x))
+    x_in = send(x_peer, n_x - 1, at_x, (lambda step: px_src.at[0], px_dst.at[0]))
+    y_idx_in = send(y_peer, n_y - 1, y_slot, (lambda step: idx_src, idx_y))
+    c_idx_in = send(core_peer, n_core - 1, at_core, (lambda step: idx_src, idx_c))
+    for mine, ref in ((my_x, idx_x), (n_z - 1, idx_z), (n_y - 1, idx_y), (my_core, idx_c)):
         ref[mine] = idx_src[...]
     px_dst[0, my_x] = px_src[0]
 
@@ -282,7 +310,10 @@
     z_idx_in()
     x_idx_in()
     need_cols = idx_z[:, 0, :].astype(F32).T[:slots]
-    own_cols = lax.broadcasted_iota(I32, (n_z * SHARE, TILE), 0) + my_x * (n_z * SHARE)
+    in_share = lax.broadcasted_iota(I32, (SHARE, TILE), 0)
+    own_cols = jnp.concatenate(
+        [in_share + (my_x * n_z + z_peer(step)[0]) * SHARE for step in range(n_z)], axis=0
+    )
     for k in range(n_x):
         have = twice(idx_x[k, 0:1])
         lanes = slice(k * TILE, (k + 1) * TILE)
@@ -301,35 +332,37 @@
     for it in range(ITERS):
         last = it + 1 == ITERS
         x_in()
-        sums = jnp.dot(
-            match_z[...],
-            px_dst[it].reshape(n_x * 2 * slots, TILE),
-            preferred_element_type=F32,
-        )
-        wanted = sums[:n_zneed].reshape(n_z, slots, TILE)
-        top = lane_top(wanted)
-        zs_src[it] = top * (1.0 / LEVELS)
-        zq_src[it] = levels_of(wanted, top)
-        zq_in = send(
+        parts = px_dst[it].reshape(n_x * 2 * slots, TILE)
+        start, zq_in = channel(
             z_peer,
             n_z - 1,
-            my_z,
-            (lambda at: zs_src.at[it, at], zs_dst.at[it]),
-            (lambda at: zq_src.at[it, at], zq_dst.at[it]),
+            z_slot,
+            (lambda step: zs_src.at[it, step], zs_dst.at[it]),
+            (lambda step: zq_src.at[it, step], zq_dst.at[it]),
         )
-        zo_src[it] = sums[n_zneed:].reshape(n_z, SHARE, TILE)
+        for low in range(0, n_z, n_z // CHUNKS):
+            high = low + n_z // CHUNKS
+            wanted = jnp.dot(
+                match_z[low * slots : high * slots], parts, preferred_element_type=F32
+            ).reshape(high - low, slots, TILE)
+            top = lane_top(wanted)
+            zs_src[it, low:high] = top * (1.0 / LEVELS)
+            zq_src[it, low:high] = levels_of(wanted, top)
+            start(low, min(high, n_z - 1))
+        sums = jnp.dot(match_z[n_zneed:], parts, preferred_element_type=F32)
+        zo_src[it] = sums.reshape(n_z, SHARE, TILE)
         if last:
-            zo_in = send(z_peer, n_z - 1, my_z, (lambda at: zo_src.at[it, at], zo_dst.at[it]))
-        zq_dst[it, my_z] = zq_src[it, my_z]
-        zs_dst[it, my_z] = zs_src[it, my_z]
-        zo_dst[it, my_z] = zo_src[it, my_z]
+            zo_in = send(z_peer, n_z - 1, z_slot, (lambda step: zo_src.at[it, step], zo_dst.at[it]))
+        zq_dst[it, n_z - 1] = zq_src[it, n_z - 1]
+        zs_dst[it, n_z - 1] = zs_src[it, n_z - 1]
+        zo_dst[it, n_z - 1] = zo_src[it, n_z - 1]
         if it > 0:
             yo_in()
             y_first = project_dual(
                 y_own + DUAL_STEP * (rhs_own - jnp.sum(yo_dst[...], axis=0)), rkind_own
             )
             mid_src[...] = y_first
-            mid_in = send(y_peer, n_y - 1, my_y, (lambda at: mid_src, mid_dst))
+            mid_in = send(y_peer, n_y - 1, at_y, (lambda step: mid_src, mid_dst))
             mid_dst[my_y] = y_first
         if it == 0:
             row_all = jnp.concatenate(
@@ -342,8 +375,9 @@
             y_idx_in()
             c_idx_in()
             need_rows = idx_y[:, 1, :].astype(F32).T[:slots]
-            own_at = lax.broadcasted_iota(I32, (n_y * SHARE, TILE), 0)
-            own_rows = (lax.div(own_at, SHARE) * n_core + my_core) * SHARE + lax.rem(own_at, SHARE)
+            own_rows = jnp.concatenate(
+                [in_share + (y * n_core + my_core) * SHARE for y in range(n_y)], axis=0
+            )
             for k in range(n_core):
                 have = twice(idx_c[k, 1:2])
                 lanes = slice(k * TILE, (k + 1) * TILE)
@@ -366,10 +400,10 @@
             upper_need,
         )
         if not last:
-            zo_in = send(z_peer, n_z - 1, my_z, (lambda at: zo_src.at[it, at], zo_dst.at[it]))
+            zo_in = send(z_peer, n_z - 1, z_slot, (lambda step: zo_src.at[it, step], zo_dst.at[it]))
         put_split(pc_src.at[it], fore((2.0 * x_new - x_need).astype(BF16).astype(F32)))
         x_need = x_new
-        c_in = send(core_peer, n_core - 1, my_core, (lambda at: pc_src.at[it], pc_dst.at[it]))
+        c_in = send(core_peer, n_core - 1, at_core, (lambda step: pc_src.at[it], pc_dst.at[it]))
         pc_dst[it, my_core] = pc_src[it]
         if last:
             zo_in()
@@ -380,36 +414,41 @@
         c_in()
         parts = pc_dst[it].reshape(n_core * 2 * slots, TILE)
         if not last:
-            sums = jnp.dot(match_y[...], parts, preferred_element_type=F32)
-            wanted = sums[:n_yneed].reshape(n_y, slots, TILE)
-            top = lane_top(wanted)
-            ys_src[...] = top * (1.0 / LEVELS)
-            yq_src[...] = levels_of(wanted, top)
-            yq_in = send(
+            start, yq_in = channel(
                 y_peer,
                 n_y - 1,
-                my_y,
-                (lambda at: ys_src.at[at], ys_dst.at[it]),
-                (lambda at: yq_src.at[at], yq_dst.at[it]),
-            )
-            yo_src[...] = sums[n_yneed:].reshape(n_y, SHARE, TILE)
-            yq_dst[it, my_y] = yq_src[my_y]
-            ys_dst[it, my_y] = ys_src[my_y]
-            yo_dst[my_y] = yo_src[my_y]
+                y_slot,
+                (lambda step: ys_src.at[step], ys_dst.at[it]),
+                (lambda step: yq_src.at[step], yq_dst.at[it]),
+            )
+            for low in range(0, n_y, n_y // CHUNKS):
+                high = low + n_y // CHUNKS
+                wanted = jnp.dot(
+                    match_y[low * slots : high * slots], parts, preferred_element_type=F32
+                ).reshape(high - low, slots, TILE)
+                top = lane_top(wanted)
+                ys_src[low:high] = top * (1.0 / LEVELS)
+                yq_src[low:high] = levels_of(wanted, top)
+                start(low, min(high, n_y - 1))
+            sums = jnp.dot(match_y[n_yneed:], parts, preferred_element_type=F32)
+            yo_src[...] = sums.reshape(n_y, SHARE, TILE)
+            yq_dst[it, n_y - 1] = yq_src[n_y - 1]
+            ys_dst[it, n_y - 1] = ys_src[n_y - 1]
+            yo_dst[n_y - 1] = yo_src[my_y]
             zo_in()
             x_own = project_primal(
                 x_own - PRIMAL_STEP * (cost_own - jnp.sum(zo_dst[it], axis=0)), kind_own, upper_own
             )
             x_total = x_total + x_own
             yq_in()
-            yo_in = send(y_peer, n_y - 1, my_y, (lambda at: yo_src.at[at], yo_dst))
+            yo_in = send(y_peer, n_y - 1, y_slot, (lambda step: yo_src.at[y_peer(step)[0]], yo_dst))
             y_need = project_dual(
                 y_need + DUAL_STEP * (rhs_need - total(yq_dst[it], ys_dst[it])), rkind_need
             )
             put_split(
                 px_src.at[it + 1], back(y_need.astype(BF16).astype(F32), lambda g: None)
             )
-            x_in = send(x_peer, n_x - 1, my_x, (lambda at: px_src.at[it + 1], px_dst.at[it + 1]))
+            x_in = send(x_peer, n_x - 1, at_x, (lambda step: px_src.at[it + 1], px_dst.at[it + 1]))
             px_dst[it + 1, my_x] = px_src[it + 1]
 
     sums = jnp.dot(match_y[n_yneed:], parts, preferred_element_type=F32)
@@ -419,16 +458,16 @@
     yq_in = send(
         y_peer,
         n_y - 1,
-        my_y,
-        (lambda at: ls_src, ys_dst.at[ITERS - 1]),
-        (lambda at: lq_src, yq_dst.at[ITERS - 1]),
+        y_slot,
+        (lambda step: ls_src, ys_dst.at[ITERS - 1]),
+        (lambda step: lq_src, yq_dst.at[ITERS - 1]),
     )
     primal_avg = x_total / ITERS
     po_src[...] = jnp.sum(cost_own * primal_avg, axis=0, keepdims=True)
-    po_in = send(y_peer, n_y - 1, my_y, (lambda at: po_src, po_dst))
-    yq_dst[ITERS - 1, my_y] = lq_src[...]
-    ys_dst[ITERS - 1, my_y] = ls_src[...]
-    po_dst[my_y] = po_src[...]
+    po_in = send(y_peer, n_y - 1, y_slot, (lambda step: po_src, po_dst))
+    yq_dst[ITERS - 1, n_y - 1] = lq_src[...]
+    ys_dst[ITERS - 1, n_y - 1] = ls_src[...]
+    po_dst[n_y - 1] = po_src[...]
     half_rhs = row_vecs[1].reshape(n_y, n_core, SHARE, TILE)
     half_kind = row_kind_full[...].reshape(n_y, n_core, SHARE, TILE)
 
@@ -450,7 +489,7 @@
     half_avg = (half_y + half_new) / ITERS
     fin_src[1:2] = jnp.sum(half_rhs * half_avg, axis=0, keepdims=True)
     me_last = me_row * n_core + my_core
-    fin_in = send(last_peer, n_last - 1, me_last, (lambda at: fin_src, fin_dst))
+    fin_in = send(last_peer, n_last - 1, lambda step: me_last, (lambda step: fin_src, fin_dst))
     fin_dst[me_last] = fin_src[...]
     last_y[0] = half_new
     last_y[1] = half_avg

time: 59.7 us -> 58.8 us (0.985)
  Pallas kernels: 58.2 us -> 57.3 us
    pallas_call x1, Pallas kernels: 57.6 us -> 56.7 us  [body(): pl.pallas_call(functools.partial(kernel, sizes), out_shape=pltpu.VMEM((5,...]
where the time goes in v5:
time: 58.8 us; the launch traced here: 58.6 us
  Pallas kernels  57.3 us (97%)
  between operations  1.29 us (2%)
    pallas_call x1, Pallas kernels, body(): pl.pallas_call(functools.partial(kernel, sizes), out_shape=pltpu.VMEM((5,...  56.7 us

profile of v5, /device:TPU:1, one launch (start us, length us, event | category | flops | bytes accessed | tf_op | source)
XLA Modules:
  0.0 58.6 jit_solution(201539563772467930)
XLA Ops:
  1.3 56.7 %pdhg.1.packed_ref = f32[5,8,128]{2,1,0:T(8,128)S(1)} custom-call(bf16[64,128,128]{2,1,0:T(8,128)(2,1)} %bitcast.15, s32[1,64]{1,0:T(1,128)} %bitcast.23, s32[1,64]{1,0:T(1,128)} %bitcast.24, s32[1,1]{1,0:T(1,128)S(6)} %copy.16.count_ref, f32[256,128]{1,0:T(8,128)} %bitcast.16, f32[256,128]{1,0:T(8,128)} %bitcast.17, s32[256,128]{1,0:T(8,128)} %bitcast.18, ...), custom_call_target="tpu_custom_call" | custom-call | tf_op jit(solution)/shard_map/pdhg/pallas_call | solution.py:588
  58.0 0.6 %unpack.1 = (f32[8,128]{1,0:T(8,128)}, f32[8,128]{1,0:T(8,128)}, f32[8,128]{1,0:T(8,128)}, f32[8,128]{1,0:T(8,128)}, f32[1,2]{1,0:T(1,128)}) custom-call(f32[5,8,128]{2,1,0:T(8,128)S(1)} %pdhg.1.packed_ref), custom_call_target="tpu_custom_call" | custom-call | tf_op jit(solution)/shard_map/unpack/pallas_call | solution.py:617
